TPU v7x, 32 devices: a whole 2x2x4 slice. The times are simulated.
32 devices in a mesh: dp: 16 (over z, y, core), fsdp: 2 (over x).
Axes of the slice: x: 2, y: 2, z: 4, core: 2. Of those that a mesh axis runs over, the one named last changes fastest.
Arguments:
- tokens: bfloat16 [32, 512, 1024], P(('dp', 'fsdp')), may hold values from -6 to 6
- cotangent: bfloat16 [32, 512, 1024], P(('dp', 'fsdp')), may hold values from -6 to 6
- doc_lengths: int32 [32, 8], P(('dp', 'fsdp')), may hold values from 1 to 256, 512 in all within a row
- expand: float32 [1024, 3072], P(('dp', 'fsdp')), may hold values from -0.1875 to 0.1875
- expand_mean: float32 [1024, 3072], P(('dp', 'fsdp')), may hold values from -0.00018310547 to 0.00018310547
- expand_square: float32 [1024, 3072], P(('dp', 'fsdp')), may hold values from 3.639278e-09 to 1.4419781e-08
- contract: float32 [1536, 1024], P(('dp', 'fsdp')), may hold values from -0.625 to 0.625
- contract_mean: float32 [1536, 1024], P(('dp', 'fsdp')), may hold values from -0.00018310547 to 0.00018310547
- contract_square: float32 [1536, 1024], P(('dp', 'fsdp')), may hold values from 3.639278e-09 to 1.4419781e-08
- gating: float32 [1536, 256], P(('dp', 'fsdp')), may hold values from -0.5 to 0.5
- gating_mean: float32 [1536, 256], P(('dp', 'fsdp')), may hold values from -0.00018310547 to 0.00018310547
- gating_square: float32 [1536, 256], P(('dp', 'fsdp')), may hold values from 3.639278e-09 to 1.4419781e-08
- widen: float32 [1024, 6144], P(('dp', 'fsdp')), may hold values from -0.1875 to 0.1875
- widen_mean: float32 [1024, 6144], P(('dp', 'fsdp')), may hold values from -0.00018310547 to 0.00018310547
- widen_square: float32 [1024, 6144], P(('dp', 'fsdp')), may hold values from 3.639278e-09 to 1.4419781e-08
- narrow: float32 [3072, 1024], P(('dp', 'fsdp')), may hold values from -0.21875 to 0.21875
- narrow_mean: float32 [3072, 1024], P(('dp', 'fsdp')), may hold values from -0.00018310547 to 0.00018310547
- narrow_square: float32 [3072, 1024], P(('dp', 'fsdp')), may hold values from 3.639278e-09 to 1.4419781e-08
- scales: float32 [1024, 2], P(('dp', 'fsdp')), may hold values from 0.2 to 2
- scales_mean: float32 [1024, 2], P(('dp', 'fsdp')), may hold values from -0.0007324219 to 0.0007324219
- scales_square: float32 [1024, 2], P(('dp', 'fsdp')), may hold values from 5.836578e-08 to 2.3346313e-07
- temporal: float32 [1536, 8], P(('dp', 'fsdp')), may hold values from -2 to 4.6, as said below
- temporal_mean: float32 [1536, 8], P(('dp', 'fsdp')), may hold values from -0.0007324219 to 0.0007324219
- temporal_square: float32 [1536, 8], P(('dp', 'fsdp')), may hold values from 5.836578e-08 to 2.3346313e-07
Outputs:
- block_out: bfloat16 [32, 512, 1024], P(('dp', 'fsdp'))
- tokens_grad: bfloat16 [32, 512, 1024], P(('dp', 'fsdp'))
- grad_norm: float32 [], replicated
- expand_after: float32 [1024, 3072], P(('dp', 'fsdp'))
- expand_means: float32 [1024, 3072], P(('dp', 'fsdp'))
- expand_squares: float32 [1024, 3072], P(('dp', 'fsdp'))
- contract_after: float32 [1536, 1024], P(('dp', 'fsdp'))
- contract_means: float32 [1536, 1024], P(('dp', 'fsdp'))
- contract_squares: float32 [1536, 1024], P(('dp', 'fsdp'))
- gating_after: float32 [1536, 256], P(('dp', 'fsdp'))
- gating_means: float32 [1536, 256], P(('dp', 'fsdp'))
- gating_squares: float32 [1536, 256], P(('dp', 'fsdp'))
- widen_after: float32 [1024, 6144], P(('dp', 'fsdp'))
- widen_means: float32 [1024, 6144], P(('dp', 'fsdp'))
- widen_squares: float32 [1024, 6144], P(('dp', 'fsdp'))
- narrow_after: float32 [3072, 1024], P(('dp', 'fsdp'))
- narrow_means: float32 [3072, 1024], P(('dp', 'fsdp'))
- narrow_squares: float32 [3072, 1024], P(('dp', 'fsdp'))
- scales_after: float32 [1024, 2], P(('dp', 'fsdp'))
- scales_means: float32 [1024, 2], P(('dp', 'fsdp'))
- scales_squares: float32 [1024, 2], P(('dp', 'fsdp'))
- temporal_after: float32 [1536, 8], P(('dp', 'fsdp'))
- temporal_means: float32 [1536, 8], P(('dp', 'fsdp'))
- temporal_squares: float32 [1536, 8], P(('dp', 'fsdp'))
Inputs may be any that keep to these rules, and one draw needn't show every extreme that they name: `doc_lengths`: each row's 8 lengths sum to 512, and each row holds a document of exactly 256 tokens. `temporal`: column 7 lies within 2.2 to 4.6.
All inputs are finite; a program needn't handle non-finite values.
Results may differ from a plain program's by a relative error of at most 0.012.
The roundings to bfloat16 on the way count: a program that leaves them out, or rounds other values in their place, can miss the bound.
Values may be sent and summed in bfloat16 or wider, within the bound.
A program may use at most 320 MiB of HBM per device.

v0:
```python
import jax
import jax.numpy as jnp
from jax import lax
from jax.sharding import PartitionSpec as P

STEP = 10


NORM_EPSILON = 1e-06
GATE_POWER = 8.0
BETA_FIRST = 0.9
BETA_SECOND = 0.95
ADAM_EPSILON = 1e-08
RATE_MATRIX = 0.1
RATE_VECTOR = 1.0
WEIGHT_DECAY = 0.1
CLIP_NORM = 1.0


def rms_scale(values, weights):
    return (
        values
        * lax.rsqrt(jnp.mean(values * values, axis=-1, keepdims=True) + NORM_EPSILON)
        * weights
    )


def doc_tables(lengths, length):
    starts = jnp.cumsum(lengths, axis=-1) - lengths
    places = jnp.arange(length, dtype=jnp.int32)
    matches = places[:, None] == starts[..., None, :]
    resets = jnp.any(matches, axis=-1).astype(jnp.float32)
    segment = jnp.sum((starts[..., None, :] <= places[:, None]).astype(jnp.int32), axis=-1)
    return (resets, segment)


def causal_conv(inputs, conv_taps, conv_bias, segment):
    length = inputs.shape[-2]
    running = conv_bias + inputs * conv_taps[:, 0]
    for offset in range(1, 4):
        shifted = jnp.concatenate(
            [jnp.zeros_like(inputs[..., :offset, :]), inputs[..., : length - offset, :]], axis=-2
        )
        earlier_segment = jnp.concatenate(
            [jnp.full_like(segment[..., :offset], -1), segment[..., : length - offset]], axis=-1
        )
        keeping = (earlier_segment == segment).astype(jnp.float32)[..., None]
        running = running + shifted * conv_taps[:, offset] * keeping
    return running


def combine_linear(earlier, later):
    return (earlier[0] * later[0], later[0] * earlier[1] + later[1])


def recurrence(decays, inputs):
    return lax.associative_scan(combine_linear, (decays, inputs), axis=-2)[1]


def temporal_mix(gate_logits, branch_logits, conv_values, recur_bias, resets):
    head_width = gate_logits.shape[-1] // 2
    flat_shape = branch_logits.shape
    recur_logit = gate_logits[..., :head_width].reshape(flat_shape) + recur_bias[:, 0]
    input_logit = gate_logits[..., head_width:].reshape(flat_shape) + recur_bias[:, 1]
    recur_gate = jax.nn.sigmoid(recur_logit)
    input_gate = jax.nn.sigmoid(input_logit)
    log_decay = -GATE_POWER * recur_gate * jax.nn.softplus(-recur_bias[:, 2])
    carried = 1.0 - resets[..., None]
    decays = jnp.exp(log_decay) * carried
    scaling = jnp.sqrt(-jnp.expm1(2.0 * log_decay)) * carried + resets[..., None]
    states = recurrence(decays, scaling * input_gate * conv_values)
    return states * jax.nn.gelu(branch_logits)


def product_rows(former, latter):
    return lax.dot_general(
        former, latter, (((0,), (0,)), ((), ())), preferred_element_type=jnp.float32
    )


def product_cols(former, latter):
    return lax.dot_general(
        former, latter, (((1,), (1,)), ((), ())), preferred_element_type=jnp.float32
    )


def adam_update(master, moment_one, moment_two, gradient, factor, rate, decay):
    clipped = gradient * factor
    new_one = BETA_FIRST * moment_one + (1.0 - BETA_FIRST) * clipped
    new_two = BETA_SECOND * moment_two + (1.0 - BETA_SECOND) * clipped * clipped
    first_hat = new_one / (1.0 - BETA_FIRST**STEP)
    second_hat = new_two / (1.0 - BETA_SECOND**STEP)
    after = master - rate * (first_hat / (jnp.sqrt(second_hat) + ADAM_EPSILON) + decay * master)
    return (after, new_one, new_two)


def shards(
    tokens,
    cotangent,
    doc_lengths,
    expand,
    expand_mean,
    expand_square,
    contract,
    contract_mean,
    contract_square,
    gating,
    gating_mean,
    gating_square,
    widen,
    widen_mean,
    widen_square,
    narrow,
    narrow_mean,
    narrow_square,
    scales,
    scales_mean,
    scales_square,
    temporal,
    temporal_mean,
    temporal_square,
):
    brain = jnp.bfloat16
    expand_full, contract_full, gating_full, scales_full, temporal_full = (
        lax.all_gather(expand.astype(brain), ("dp", "fsdp"), axis=0, tiled=True),
        lax.all_gather(contract.astype(brain), ("dp", "fsdp"), axis=0, tiled=True),
        lax.all_gather(gating.astype(brain), ("dp", "fsdp"), axis=0, tiled=True),
        lax.all_gather(scales.astype(brain), ("dp", "fsdp"), axis=0, tiled=True),
        lax.all_gather(temporal.astype(brain), ("dp", "fsdp"), axis=0, tiled=True),
    )
    widen_full, narrow_full = (
        lax.all_gather(widen.astype(brain), ("dp", "fsdp"), axis=0, tiled=True),
        lax.all_gather(narrow.astype(brain), ("dp", "fsdp"), axis=0, tiled=True),
    )
    width = contract_full.shape[0]
    hidden = narrow_full.shape[0]
    head_width = gating_full.shape[1] // 2
    head_count = width // head_width
    length = tokens.shape[1]
    resets, segment = doc_tables(doc_lengths, length)
    resets = resets[0]
    segment = segment[0]
    inputs = tokens[0].astype(jnp.float32)
    scales_float = scales_full.astype(jnp.float32)
    temporal_float = temporal_full.astype(jnp.float32)
    normed, norm_pull = jax.vjp(rms_scale, inputs, scales_float[:, 0])
    normed_low = normed.astype(brain)
    projected = jnp.dot(normed_low, expand_full, preferred_element_type=jnp.float32)

    def conv_piece(values, conv_taps, conv_bias):
        return causal_conv(values, conv_taps, conv_bias, segment)

    conv_out, conv_pull = jax.vjp(
        conv_piece, projected[:, :width], temporal_float[:, 0:4], temporal_float[:, 4]
    )
    conv_low = conv_out.astype(brain)
    blocks = conv_low.reshape(length, head_count, head_width)
    gate_logits = jnp.einsum(
        "lhk,hkj->lhj",
        blocks,
        gating_full.reshape(head_count, head_width, 2 * head_width),
        preferred_element_type=jnp.float32,
    )

    def mix_piece(logits, branch_logits, conv_values, recur_bias):
        return temporal_mix(logits, branch_logits, conv_values, recur_bias, resets)

    mixed, mix_pull = jax.vjp(
        mix_piece,
        gate_logits,
        projected[:, width:],
        conv_low.astype(jnp.float32),
        temporal_float[:, 5:8],
    )
    mixed_low = mixed.astype(brain)
    middle = inputs + jnp.dot(mixed_low, contract_full, preferred_element_type=jnp.float32)
    normed_two, norm_two_pull = jax.vjp(rms_scale, middle, scales_float[:, 1])
    normed_two_low = normed_two.astype(brain)
    widened = jnp.dot(normed_two_low, widen_full, preferred_element_type=jnp.float32)

    def gated_piece(values):
        return jax.nn.gelu(values[:, :hidden]) * values[:, hidden:]

    activated, gated_pull = jax.vjp(gated_piece, widened)
    activated_low = activated.astype(brain)
    block_out = (
        middle + jnp.dot(activated_low, narrow_full, preferred_element_type=jnp.float32)
    ).astype(brain)
    widen_full, narrow_full = (
        lax.all_gather(widen.astype(brain), ("dp", "fsdp"), axis=0, tiled=True),
        lax.all_gather(narrow.astype(brain), ("dp", "fsdp"), axis=0, tiled=True),
    )
    upstream = cotangent[0]
    narrow_grad = product_rows(activated_low, upstream)
    activated_grad = product_cols(upstream, narrow_full)
    widened_grad = gated_pull(activated_grad)[0].astype(brain)
    widen_grad = product_rows(normed_two_low, widened_grad)
    normed_two_grad = product_cols(widened_grad, widen_full)
    middle_norm_grad, scale_two_grad = norm_two_pull(normed_two_grad)
    middle_grad = upstream.astype(jnp.float32) + middle_norm_grad
    expand_full, contract_full, gating_full = (
        lax.all_gather(expand.astype(brain), ("dp", "fsdp"), axis=0, tiled=True),
        lax.all_gather(contract.astype(brain), ("dp", "fsdp"), axis=0, tiled=True),
        lax.all_gather(gating.astype(brain), ("dp", "fsdp"), axis=0, tiled=True),
    )
    middle_low = middle_grad.astype(brain)
    contract_grad = product_rows(mixed_low, middle_low)
    mixed_grad = product_cols(middle_low, contract_full)
    logit_grad, branch_grad, conv_mix_grad, recur_bias_grad = mix_pull(mixed_grad)
    logit_low = logit_grad.astype(brain)
    gating_blocks = gating_full.reshape(head_count, head_width, 2 * head_width)
    gating_grad = jnp.einsum(
        "lhk,lhj->hkj", blocks, logit_low, preferred_element_type=jnp.float32
    ).reshape(width, 2 * head_width)
    conv_grad = conv_mix_grad + jnp.einsum(
        "lhj,hkj->lhk", logit_low, gating_blocks, preferred_element_type=jnp.float32
    ).reshape(length, width)
    input_grad, taps_grad, conv_bias_grad = conv_pull(conv_grad)
    projected_low = jnp.concatenate([input_grad, branch_grad], axis=1).astype(brain)
    expand_grad = product_rows(normed_low, projected_low)
    normed_grad = product_cols(projected_low, expand_full)
    token_norm_grad, scale_one_grad = norm_pull(normed_grad)
    tokens_grad = (middle_grad + token_norm_grad).astype(brain)
    scales_grad = jnp.stack([scale_one_grad, scale_two_grad], axis=1)
    temporal_grad = jnp.concatenate([taps_grad, conv_bias_grad[:, None], recur_bias_grad], axis=1)
    summed = (
        lax.psum_scatter(expand_grad, ("dp", "fsdp"), scatter_dimension=0, tiled=True),
        lax.psum_scatter(contract_grad, ("dp", "fsdp"), scatter_dimension=0, tiled=True),
        lax.psum_scatter(gating_grad, ("dp", "fsdp"), scatter_dimension=0, tiled=True),
        lax.psum_scatter(widen_grad, ("dp", "fsdp"), scatter_dimension=0, tiled=True),
        lax.psum_scatter(narrow_grad, ("dp", "fsdp"), scatter_dimension=0, tiled=True),
        lax.psum_scatter(scales_grad, ("dp", "fsdp"), scatter_dimension=0, tiled=True),
        lax.psum_scatter(temporal_grad, ("dp", "fsdp"), scatter_dimension=0, tiled=True),
    )
    local_squares = jnp.float32(0.0)
    for piece in summed:
        local_squares = local_squares + jnp.sum(piece * piece)
    grad_norm = jnp.sqrt(lax.psum(local_squares, ("dp", "fsdp")))
    factor = CLIP_NORM / jnp.maximum(grad_norm, CLIP_NORM)
    masters = (expand, contract, gating, widen, narrow, scales, temporal)
    moments = (
        (expand_mean, expand_square),
        (contract_mean, contract_square),
        (gating_mean, gating_square),
        (widen_mean, widen_square),
        (narrow_mean, narrow_square),
        (scales_mean, scales_square),
        (temporal_mean, temporal_square),
    )
    updated = []
    for index in range(7):
        rate = RATE_MATRIX if index < 5 else RATE_VECTOR
        decay = WEIGHT_DECAY if index < 5 else 0.0
        updated.append(
            adam_update(
                masters[index],
                moments[index][0],
                moments[index][1],
                summed[index],
                factor,
                rate,
                decay,
            )
        )
    return (
        block_out[None],
        tokens_grad[None],
        grad_norm,
        updated[0][0],
        updated[0][1],
        updated[0][2],
        updated[1][0],
        updated[1][1],
        updated[1][2],
        updated[2][0],
        updated[2][1],
        updated[2][2],
        updated[3][0],
        updated[3][1],
        updated[3][2],
        updated[4][0],
        updated[4][1],
        updated[4][2],
        updated[5][0],
        updated[5][1],
        updated[5][2],
        updated[6][0],
        updated[6][1],
        updated[6][2],
    )


def solution(mesh):
    placed = (
        P(("dp", "fsdp"), None, None),
        P(("dp", "fsdp"), None, None),
        P(("dp", "fsdp"), None),
        P(("dp", "fsdp"), None),
        P(("dp", "fsdp"), None),
        P(("dp", "fsdp"), None),
        P(("dp", "fsdp"), None),
        P(("dp", "fsdp"), None),
        P(("dp", "fsdp"), None),
        P(("dp", "fsdp"), None),
        P(("dp", "fsdp"), None),
        P(("dp", "fsdp"), None),
        P(("dp", "fsdp"), None),
        P(("dp", "fsdp"), None),
        P(("dp", "fsdp"), None),
        P(("dp", "fsdp"), None),
        P(("dp", "fsdp"), None),
        P(("dp", "fsdp"), None),
        P(("dp", "fsdp"), None),
        P(("dp", "fsdp"), None),
        P(("dp", "fsdp"), None),
        P(("dp", "fsdp"), None),
        P(("dp", "fsdp"), None),
        P(("dp", "fsdp"), None),
    )
    return jax.shard_map(
        shards,
        mesh=mesh,
        in_specs=placed,
        out_specs=(
            P(("dp", "fsdp"), None, None),
            P(("dp", "fsdp"), None, None),
            P(),
            P(("dp", "fsdp"), None),
            P(("dp", "fsdp"), None),
            P(("dp", "fsdp"), None),
            P(("dp", "fsdp"), None),
            P(("dp", "fsdp"), None),
            P(("dp", "fsdp"), None),
            P(("dp", "fsdp"), None),
            P(("dp", "fsdp"), None),
            P(("dp", "fsdp"), None),
            P(("dp", "fsdp"), None),
            P(("dp", "fsdp"), None),
            P(("dp", "fsdp"), None),
            P(("dp", "fsdp"), None),
            P(("dp", "fsdp"), None),
            P(("dp", "fsdp"), None),
            P(("dp", "fsdp"), None),
            P(("dp", "fsdp"), None),
            P(("dp", "fsdp"), None),
            P(("dp", "fsdp"), None),
            P(("dp", "fsdp"), None),
            P(("dp", "fsdp"), None),
        ),
        check_vma=False,
    )
```

profile of v0, /device:TPU:0, one launch (start us, length us, event | category | flops | bytes accessed | tf_op | source)
XLA Modules:
  0.0 2025.8 jit_solution(9801610329896653421)
XLA Ops:
  15.4 69.7 %all-gather.1 = bf16[32,32,2]{1,2,0:T(2,128)(2,1)S(1)} all-gather(bf16[1,32,2]{1,2,0:T(2,128)(2,1)S(1)} %convert_bitcast_fusion.1), channel_id=1, replica_groups=mesh['dp'=16,'fsdp'=2] {'dp','fsdp'}, dimensions={0}, use_global_device_ids=true | all-gather | bytes 4224 | tf_op jit(solution)/shard_map/all_gather | solution.py:128
  85.2 64.1 %all-gather = bf16[32,48,8]{1,2,0:T(8,128)(2,1)S(1)} all-gather(bf16[1,48,8]{1,2,0:T(8,128)(2,1)S(1)} %convert_bitcast_fusion), channel_id=1, replica_groups=mesh['dp'=16,'fsdp'=2] {'dp','fsdp'}, dimensions={0}, use_global_device_ids=true | all-gather | bytes 25344 | tf_op jit(solution)/shard_map/all_gather | solution.py:129
  150.3 79.1 %all_gather.29 = bf16[1536,256]{1,0:T(8,128)(2,1)} all-gather(bf16[48,256]{1,0:T(8,128)(2,1)S(1)} %convert_element_type.125), channel_id=1, replica_groups=mesh['dp'=16,'fsdp'=2] {'dp','fsdp'}, dimensions={0}, use_global_device_ids=true | all-gather | bytes 811008 | tf_op jit(solution)/shard_map/all_gather | solution.py:127
  256.4 7.5 exponential_multiply_fusion
  348.5 7.3 slice.380
  355.8 7.3 slice.445
  492.5 9.7 pad.395
  502.2 9.6 pad.396
  511.8 7.3 multiply_convert_fusion.1
  525.1 14.6 fusion.87
  539.7 16.0 fusion.17
  555.7 15.5 multiply_reduce_fusion.5
  672.6 9.8 pad.401
  809.7 9.7 pad.458
  829.8 9.6 pad.457
  846.5 9.7 pad.483
  856.1 9.8 pad.484
  866.0 9.9 pad.460
  876.0 10.8 multiply_reduce_fusion
  910.5 7.8 multiply_reduce_fusion.4
  946.2 8.0 fusion.25
  955.4 8.5 fusion.31
  965.5 16.6 fusion.35
  983.4 8.8 fusion.28
  992.2 70.0 %reduce-scatter.22.cloned.1.call-done = f32[32,2]{1,0:T(8,128)} async-done(((f32[1024,2]{1,0:T(8,128)}), f32[32,2]{1,0:T(8,128)}) %reduce-scatter.22.cloned.1.call-update) | async-done | bytes 272
  1063.6 96.3 %reduce-scatter.24.cloned.1.call-done = f32[48,8]{1,0:T(8,128)} async-done(((f32[1536,8]{1,0:T(8,128)}), f32[48,8]{1,0:T(8,128)}) %reduce-scatter.24.cloned.1.call-update) | async-done | bytes 1552
  1161.4 100.8 %reduce-scatter.16.cloned.1.call-done = f32[48,256]{1,0:T(8,128)} async-done(((f32[1536,256]{1,0:T(8,128)}), f32[48,256]{1,0:T(8,128)}) %reduce-scatter.16.cloned.1.call-update) | async-done | bytes 49168 | tf_op jit(solution)/shard_map/reduce_scatter | solution.py:229
  1263.5 118.8 %reduce-scatter.14.cloned.1.call-done = f32[48,1024]{1,0:T(8,128)} async-done(((f32[1536,1024]{1,0:T(8,128)}), f32[48,1024]{1,0:T(8,128)}) %reduce-scatter.14.cloned.1.call-update) | async-done | bytes 196624 | tf_op jit(solution)/shard_map/reduce_scatter | solution.py:228
  1383.9 159.4 %reduce-scatter.12.cloned.1.call-done = f32[32,3072]{1,0:T(8,128)} async-done(((f32[1024,3072]{1,0:T(8,128)}), f32[32,3072]{1,0:T(8,128)}) %reduce-scatter.12.cloned.1.call-update) | async-done | bytes 393232 | tf_op jit(solution)/shard_map/reduce_scatter | solution.py:227
  1547.0 158.1 %reduce-scatter.20.cloned.1.call-done = f32[96,1024]{1,0:T(8,128)} async-done(((f32[3072,1024]{1,0:T(8,128)}), f32[96,1024]{1,0:T(8,128)}) %reduce-scatter.20.cloned.1.call-update) | async-done | bytes 393232 | tf_op jit(solution)/shard_map/reduce_scatter | solution.py:231
  1706.8 249.2 %reduce-scatter.18.cloned.1.call-done = f32[32,6144]{1,0:T(8,128)} async-done(((f32[1024,6144]{1,0:T(8,128)}), f32[32,6144]{1,0:T(8,128)}) %reduce-scatter.18.cloned.1.call-update) | async-done | bytes 786448 | tf_op jit(solution)/shard_map/reduce_scatter | solution.py:230
  1963.8 40.1 %psum.7 = f32[]{:T(128)} all-reduce(f32[]{:T(128)S(6)} %add.598), channel_id=1, replica_groups=mesh['dp'=16,'fsdp'=2] {'dp','fsdp'}, use_global_device_ids=true, to_apply=%region_31.32 | all-reduce | flops 1 | bytes 8 | tf_op jit(solution)/shard_map/psum | solution.py:238
  (503 shorter events, 584.2 us)
Async XLA Ops:
  7.2 78.0 %copy-start.51 = (f32[48,256]{1,0:T(8,128)S(1)}, f32[48,256]{1,0:T(8,128)}, u32[]{:S(2)}) copy-start(f32[48,256]{1,0:T(8,128)} %param.33) | copy-start | bytes 147460
  7.2 222.3 %all-gather.7.cloned.1.call-start = ((), (), s32[]{:S(2)}) async-start(), calls=%async_computation.7 | async-start | bytes 6488064 | tf_op jit(solution)/shard_map/all_gather | solution.py:125
  9.1 510.0 %all-gather.9.cloned.1.call-start = ((), (), s32[]{:S(2)}) async-start(), calls=%async_computation.8 | async-start | bytes 3244032 | tf_op jit(solution)/shard_map/all_gather | solution.py:126
  10.7 514.3 %all-gather.11.cloned.1.call-start = ((), (), s32[]{:S(2)}) async-start(), calls=%async_computation.9 | async-start | bytes 12976128 | tf_op jit(solution)/shard_map/all_gather | solution.py:132
  12.8 527.0 %all-gather.13.cloned.1.call-start = ((), (), s32[]{:S(2)}) async-start(), calls=%async_computation.10 | async-start | bytes 6488064 | tf_op jit(solution)/shard_map/all_gather | solution.py:133
  14.5 1047.7 %reduce-scatter.22.cloned.1.call-start = ((), (), s32[]{:S(2)}) async-start(), calls=%async_computation.16 | async-start | bytes 540672
  15.0 241.4 %copy-start.64 = (f32[512]{0:T(512)}, f32[512]{0:T(512)S(1)}, u32[]{:S(2)}) copy-start(f32[512]{0:T(512)S(1)} %broadcast_subtract_fusion) | copy-start | bytes 6148
  15.0 241.4 %copy-start.67 = (f32[512]{0:T(512)}, f32[512]{0:T(512)S(1)}, u32[]{:S(2)}) copy-start(f32[512]{0:T(512)S(1)} %convert_element_type.126) | copy-start | bytes 6148
  15.3 69.8 %copy-start.72 = (f32[512]{0:T(512)}, f32[512]{0:T(512)S(1)}, u32[]{:S(2)}) copy-start(f32[512]{0:T(512)S(1)} %fusion.23) | copy-start | bytes 6148
  15.3 219.9 %copy-start.39 = (f32[512]{0:T(512)}, f32[512]{0:T(512)S(1)}, u32[]{:S(2)}) copy-start(f32[512]{0:T(512)S(1)} %fusion.69) | copy-start | bytes 6148
  85.2 150.1 %copy-start.34 = (f32[1024,1]{0,1:T(1,128)}, f32[1024,1]{0,1:T(1,128)S(1)}, u32[]{:S(2)}) copy-start(f32[1024,1]{0,1:T(1,128)S(1)} %get-tuple-element.185) | copy-start | bytes 12292
  85.2 486.0 %copy-start.36 = (f32[1024,1]{0,1:T(1,128)}, f32[1024,1]{0,1:T(1,128)S(1)}, u32[]{:S(2)}) copy-start(f32[1024,1]{0,1:T(1,128)S(1)} %get-tuple-element.184) | copy-start | bytes 12292
  149.5 85.8 %copy-start.38 = (f32[1536,8]{0,1:T(8,128)}, f32[1536,8]{0,1:T(8,128)S(1)}, u32[]{:S(2)}) copy-start(f32[1536,8]{0,1:T(8,128)S(1)} %reshape.300) | copy-start | bytes 147460
  149.7 86.5 %copy-start.56 = (f32[1536]{0:T(1024)}, f32[1536]{0:T(1024)S(1)}, u32[]{:S(2)}) copy-start(f32[1536]{0:T(1024)S(1)} %get-tuple-element.36) | copy-start | bytes 18436
  149.7 86.5 %copy-start.58 = (f32[1536]{0:T(1024)}, f32[1536]{0:T(1024)S(1)}, u32[]{:S(2)}) copy-start(f32[1536]{0:T(1024)S(1)} %get-tuple-element.33) | copy-start | bytes 18436
  149.7 86.5 %copy-start.60 = (f32[1536]{0:T(1024)}, f32[1536]{0:T(1024)S(1)}, u32[]{:S(2)}) copy-start(f32[1536]{0:T(1024)S(1)} %get-tuple-element.35) | copy-start | bytes 18436
  149.7 86.5 %copy-start.62 = (f32[1536]{0:T(1024)}, f32[1536]{0:T(1024)S(1)}, u32[]{:S(2)}) copy-start(f32[1536]{0:T(1024)S(1)} %get-tuple-element.34) | copy-start | bytes 18436
  149.7 106.7 %copy-start.43 = (f32[1536]{0:T(1024)}, f32[1536]{0:T(1024)S(1)}, u32[]{:S(2)}) copy-start(f32[1536]{0:T(1024)S(1)} %get-tuple-element.30) | copy-start | bytes 18436
  149.7 106.7 %copy-start.45 = (f32[1536]{0:T(1024)}, f32[1536]{0:T(1024)S(1)}, u32[]{:S(2)}) copy-start(f32[1536]{0:T(1024)S(1)} %get-tuple-element.31) | copy-start | bytes 18436
  150.3 106.1 %copy-start.47 = (f32[1536]{0:T(1024)}, f32[1536]{0:T(1024)S(1)}, u32[]{:S(2)}) copy-start(f32[1536]{0:T(1024)S(1)} %get-tuple-element.183) | copy-start | bytes 18436
  690.6 51.6 %slice-start.6 = ((f32[16,1536]{1,0:T(8,128)}), f32[1,1536]{1,0:T(1,128)S(1)}, s32[]{:S(2)}) async-start(f32[16,1536]{1,0:T(8,128)} %slice.458), calls=%async_computation.24 | async-start | bytes 12288 | tf_op jit(solution)/shard_map/transpose(jvp())/split | solution.py:57
  931.7 228.3 %reduce-scatter.24.cloned.1.call-start = ((), (), s32[]{:S(2)}) async-start(), calls=%async_computation.17 | async-start | bytes 811008
  933.0 329.2 %reduce-scatter.16.cloned.1.call-start = ((), (), s32[]{:S(2)}) async-start(), calls=%async_computation.13 | async-start | bytes 1622016 | tf_op jit(solution)/shard_map/reduce_scatter | solution.py:229
  937.8 444.5 %reduce-scatter.14.cloned.1.call-start = ((), (), s32[]{:S(2)}) async-start(), calls=%async_computation.12 | async-start | bytes 6488064 | tf_op jit(solution)/shard_map/reduce_scatter | solution.py:228
  944.5 598.9 %reduce-scatter.12.cloned.1.call-start = ((), (), s32[]{:S(2)}) async-start(), calls=%async_computation.11 | async-start | bytes 12976128 | tf_op jit(solution)/shard_map/reduce_scatter | solution.py:227
  954.2 750.9 %reduce-scatter.20.cloned.1.call-start = ((), (), s32[]{:S(2)}) async-start(), calls=%async_computation.15 | async-start | bytes 12976128 | tf_op jit(solution)/shard_map/reduce_scatter | solution.py:231
  963.9 992.1 %reduce-scatter.18.cloned.1.call-start = ((), (), s32[]{:S(2)}) async-start(), calls=%async_computation.14 | async-start | bytes 25952256 | tf_op jit(solution)/shard_map/reduce_scatter | solution.py:230
  983.4 977.2 %copy-start.14 = (f32[512,1024]{1,0:T(8,128)S(1)}, f32[512,1024]{1,0:T(8,128)}, u32[]{:S(2)}) copy-start(f32[512,1024]{1,0:T(8,128)} %copy-done.13) | copy-start | bytes 6291460
  1063.0 897.5 %copy-start.82 = (f32[32,2]{0,1:T(2,128)}, f32[32,2]{0,1:T(2,128)S(1)}, u32[]{:S(2)}) copy-start(f32[32,2]{0,1:T(2,128)S(1)} %copy.121) | copy-start | bytes 772
  1960.6 50.5 %copy-start.28 = (f32[96,1024]{1,0:T(8,128)S(1)}, f32[96,1024]{1,0:T(8,128)}, u32[]{:S(2)}) copy-start(f32[96,1024]{1,0:T(8,128)} %param.39) | copy-start | bytes 1179652
  1963.8 49.8 %copy-start.29 = (f32[32,3072]{1,0:T(8,128)S(1)}, f32[32,3072]{1,0:T(8,128)}, u32[]{:S(2)}) copy-start(f32[32,3072]{1,0:T(8,128)} %param.27) | copy-start | bytes 1179652
  1963.8 49.8 %copy-start.30 = (f32[32,3072]{1,0:T(8,128)S(1)}, f32[32,3072]{1,0:T(8,128)}, u32[]{:S(2)}) copy-start(f32[32,3072]{1,0:T(8,128)} %reduce-scatter.12.cloned.1.call-done) | copy-start | bytes 1179652
  (77 other events, 627.8 us)
Sparse Core Ops, SparseCore 0:
  11.5 72.3 all-gather.6
  86.9 57.6 all-gather.8
  147.4 99.2 all-gather.10
  249.5 70.8 all-gather.12
  931.8 130.3 reduce-scatter.21
  1068.5 91.3 reduce-scatter.23
  1166.0 96.0 reduce-scatter.15
  1268.7 113.5 reduce-scatter.13
  1388.4 154.9 reduce-scatter.11
  1550.3 154.7 reduce-scatter.19
  1711.5 244.4 reduce-scatter.17
where the time goes:
time: 2050 us; the launch traced here: 2030 us
  waiting for transfers between devices  953 us (46%)
  local copies, waits for them, and re-layouts  457 us (22%)
  blocking collectives  253 us (12%)
  other arithmetic  210 us (10%)
  matrix products  130 us (6%)
  between operations  22 us (1%)
    reduce_scatter x1, waiting for transfers between devices, shards(): lax.psum_scatter(widen_grad, ('dp', 'fsdp'), scatter_dimension=0, tiled=T...  249 us
    pad x70, local copies, waits for them, and re-layouts, recurrence(): return lax.associative_scan(combine_linear, (decays, inputs), axis=-2)[1]  234 us
    slice x69, local copies, waits for them, and re-layouts, recurrence(): return lax.associative_scan(combine_linear, (decays, inputs), axis=-2)[1]  180 us
    unnamed x13, waiting for transfers between devices  167 us
    reduce_scatter x1, waiting for transfers between devices, shards(): lax.psum_scatter(expand_grad, ('dp', 'fsdp'), scatter_dimension=0, tiled=...  159 us
    reduce_scatter x1, waiting for transfers between devices, shards(): lax.psum_scatter(narrow_grad, ('dp', 'fsdp'), scatter_dimension=0, tiled=...  158 us
    reduce_scatter x1, waiting for transfers between devices, shards(): lax.psum_scatter(contract_grad, ('dp', 'fsdp'), scatter_dimension=0, tile...  119 us
    reduce_scatter x1, waiting for transfers between devices, shards(): lax.psum_scatter(gating_grad, ('dp', 'fsdp'), scatter_dimension=0, tiled=...  101 us
  transfers between devices with their start and end apart: 11, of which 7 were waited for; matrix products, arithmetic and copies ran while one was open for 19% of the time, Pallas kernels for 0%

commit v1 on v0

--- a/solution.py
+++ b/solution.py
@@ -1,6 +1,10 @@
+import functools
+
 import jax
 import jax.numpy as jnp
 from jax import lax
+from jax.experimental import pallas as pl
+from jax.experimental.pallas import tpu as pltpu
 from jax.sharding import PartitionSpec as P
 
 STEP = 10
@@ -15,6 +19,351 @@
 RATE_VECTOR = 1.0
 WEIGHT_DECAY = 0.1
 CLIP_NORM = 1.0
+
+
+MESH = pl.DeviceIdType.MESH
+BRAIN = jnp.bfloat16
+VMEM_BYTES = 60 * 1024 * 1024
+
+
+def bit_count(size):
+    return size.bit_length() - 1
+
+
+class Cube:
+    def __init__(self, mesh_shape):
+        self.dp = bit_count(mesh_shape["dp"])
+        self.fsdp = bit_count(mesh_shape["fsdp"])
+        self.bits = self.dp + self.fsdp
+        self.core = self.dp - 1
+
+    def place(self):
+        outer, inner = lax.axis_index("dp"), lax.axis_index("fsdp")
+        bits = [lax.rem(outer // (1 << (self.dp - 1 - i)), 2) for i in range(self.dp)]
+        return bits + [lax.rem(inner // (1 << (self.fsdp - 1 - i)), 2) for i in range(self.fsdp)]
+
+    def partner(self, place, bit):
+        outer, inner = lax.axis_index("dp"), lax.axis_index("fsdp")
+        flip = 1 - 2 * place[bit]
+        if bit < self.dp:
+            return (outer + flip * (1 << (self.dp - 1 - bit)), inner)
+        return (outer, inner + flip * (1 << (self.bits - 1 - bit)))
+
+    def orders(self):
+        rest = [i for i in range(self.bits) if i != self.core]
+        last = rest[-1]
+        across = rest[-2]
+        lines = rest[:-2]
+        return [
+            [last] + lines + [across, self.core],
+            [across] + lines + [last, self.core],
+            lines + [across, last, self.core],
+            lines + [last, across, self.core],
+        ]
+
+
+def greet(cube, place):
+    barrier = pltpu.get_barrier_semaphore()
+    for bit in range(cube.bits):
+        pl.semaphore_signal(barrier, inc=1, device_id=cube.partner(place, bit), device_id_type=MESH)
+    pl.semaphore_wait(barrier, cube.bits)
+
+
+def cut_pieces(cube, widths, groups):
+    orders = cube.orders()
+    pieces = []
+    for array, width in enumerate(widths):
+        first = 0
+        for group, share in groups[array]:
+            for columns, order in zip(share, orders):
+                if columns:
+                    pieces.append((group, array, first, columns * 128, order))
+                    first += columns * 128
+        assert first == width
+    return sorted(pieces, key=lambda piece: piece[0])
+
+
+def gather_kernel(cube, pieces, count, *refs):
+    sources, fulls = refs[:count], refs[count : 2 * count]
+    held, own_sem, send_sem, recv_sem = (
+        refs[2 * count : 3 * count],
+        refs[3 * count],
+        refs[3 * count + 1],
+        refs[3 * count + 2],
+    )
+    place = cube.place()
+    greet(cube, place)
+    own = []
+    for i in range(count):
+        held[i][...] = sources[i][...].astype(held[i].dtype)
+        copy = pltpu.make_async_copy(held[i], fulls[i].at[tuple(place)], own_sem.at[i])
+        copy.start()
+        own.append(copy)
+    for copy in own:
+        copy.wait()
+
+    def exchange(number, stage):
+        _, array, first, columns, order = pieces[number]
+        spot = tuple(
+            slice(None) if bit in order[:stage] else place[bit] for bit in range(cube.bits)
+        )
+        view = fulls[array].at[spot + (slice(None), pl.ds(first, columns))]
+        return pltpu.make_async_remote_copy(
+            src_ref=view,
+            dst_ref=view,
+            send_sem=send_sem.at[number, stage],
+            recv_sem=recv_sem.at[number, stage],
+            device_id=cube.partner(place, order[stage]),
+            device_id_type=MESH,
+        )
+
+    for slot in range(pieces[-1][0] + cube.bits + 1):
+        for number in range(len(pieces)):
+            stage = slot - pieces[number][0]
+            if 0 <= stage <= cube.bits:
+                if stage > 0:
+                    exchange(number, stage - 1).wait_recv()
+                if stage < cube.bits:
+                    exchange(number, stage).start()
+    for number in range(len(pieces)):
+        for stage in range(cube.bits):
+            exchange(number, stage).wait_send()
+
+
+def gather_all(cube, shards_in, kinds, groups):
+    count = len(shards_in)
+    pieces = cut_pieces(cube, [s.shape[1] for s in shards_in], groups)
+    fulls = [(2,) * cube.bits + s.shape for s in shards_in]
+    gathered = pl.pallas_call(
+        functools.partial(gather_kernel, cube, pieces, count),
+        out_shape=[jax.ShapeDtypeStruct(shape, kind) for shape, kind in zip(fulls, kinds)],
+        in_specs=[pl.BlockSpec(memory_space=pltpu.VMEM)] * count,
+        out_specs=[pl.BlockSpec(memory_space=pl.ANY)] * count,
+        scratch_shapes=[pltpu.VMEM(s.shape, kind) for s, kind in zip(shards_in, kinds)]
+        + [
+            pltpu.SemaphoreType.DMA((count,)),
+            pltpu.SemaphoreType.DMA((len(pieces), cube.bits)),
+            pltpu.SemaphoreType.DMA((len(pieces), cube.bits)),
+        ],
+        compiler_params=pltpu.CompilerParams(
+            collective_id=0, has_side_effects=True, vmem_limit_bytes=VMEM_BYTES
+        ),
+    )(*shards_in)
+    return [g.reshape((-1,) + g.shape[cube.bits + 1 :]) for g in gathered]
+
+
+def scatter_kernel(cube, pieces, count, *refs):
+    grads, sums = refs[:count], refs[count : 2 * count]
+    norm = refs[2 * count]
+    refs = refs[2 * count + 1 :]
+    held = refs[:count]
+    inbox = [
+        refs[(1 + stage) * count : (2 + stage) * count] for stage in range(cube.bits)
+    ]
+    own_sem, send_sem, recv_sem, partial, other, norm_send, norm_recv = refs[
+        (1 + cube.bits) * count :
+    ]
+    place = cube.place()
+    greet(cube, place)
+
+    def bits_left(number, stage):
+        order = pieces[number][4]
+        return [bit for bit in range(cube.bits) if bit not in order[cube.bits - stage :]]
+
+    def own_copy(number):
+        _, array, first, columns, order = pieces[number]
+        spot = tuple(place[bit] if bit == order[-1] else slice(None) for bit in range(cube.bits))
+        window = (slice(None), pl.ds(first, columns))
+        rest = (slice(None),) * (cube.bits - 1)
+        return pltpu.make_async_copy(
+            grads[array].at[spot + window], held[array].at[rest + window], own_sem.at[number]
+        )
+
+    def exchange(number, stage):
+        _, array, first, columns, order = pieces[number]
+        bit = order[cube.bits - 1 - stage]
+        left = bits_left(number, stage)
+        source = grads[array] if stage == 0 else inbox[stage - 1][array]
+        spot = tuple(1 - place[bit] if b == bit else slice(None) for b in left)
+        window = (slice(None), pl.ds(first, columns))
+        rest = (slice(None),) * (len(left) - 1)
+        return pltpu.make_async_remote_copy(
+            src_ref=source.at[spot + window],
+            dst_ref=inbox[stage][array].at[rest + window],
+            send_sem=send_sem.at[number, stage],
+            recv_sem=recv_sem.at[number, stage],
+            device_id=cube.partner(place, bit),
+            device_id_type=MESH,
+        )
+
+    def add(number, stage):
+        _, array, first, columns, order = pieces[number]
+        bit = order[cube.bits - 1 - stage]
+        left = bits_left(number, stage)
+        after = [b for b in left if b != bit]
+        window = (slice(None), pl.ds(first, columns))
+        target = inbox[stage][array]
+
+        def one(step, carry):
+            spot = tuple(
+                lax.rem(step // (1 << (len(after) - 1 - i)), 2) for i in range(len(after))
+            )
+            if stage == 0:
+                mine = held[array][spot + window]
+            else:
+                mixed = list(spot)
+                mixed.insert(left.index(bit), place[bit])
+                mine = inbox[stage - 1][array][tuple(mixed) + window]
+            total = mine.astype(jnp.float32) + target[spot + window].astype(jnp.float32)
+            if stage == cube.bits - 1:
+                sums[array][window] = total
+                squares = total * total
+                tile = squares.reshape(squares.shape[0] // 8, 8, columns).sum(axis=0)
+                for start in range(0, columns, 128):
+                    partial[0] += tile[:, start : start + 128]
+            else:
+                target[spot + window] = total.astype(target.dtype)
+            return carry
+
+        lax.fori_loop(0, 1 << len(after), one, 0)
+
+    partial[0] = jnp.zeros(partial.shape[1:], jnp.float32)
+    for number in range(len(pieces)):
+        own_copy(number).start()
+    for slot in range(pieces[-1][0] + cube.bits + 1):
+        for number in range(len(pieces)):
+            stage = slot - pieces[number][0]
+            if 0 <= stage <= cube.bits:
+                if stage > 0:
+                    if stage == 1:
+                        own_copy(number).wait()
+                    exchange(number, stage - 1).wait_recv()
+                    add(number, stage - 1)
+                if stage < cube.bits:
+                    exchange(number, stage).start()
+    for number in range(len(pieces)):
+        for stage in range(cube.bits):
+            exchange(number, stage).wait_send()
+    for bit in range(cube.bits):
+        copy = pltpu.make_async_remote_copy(
+            src_ref=partial.at[bit],
+            dst_ref=other.at[bit],
+            send_sem=norm_send.at[bit],
+            recv_sem=norm_recv.at[bit],
+            device_id=cube.partner(place, bit),
+            device_id_type=MESH,
+        )
+        copy.start()
+        copy.wait()
+        if bit < cube.bits - 1:
+            partial[bit + 1] = partial[bit] + other[bit]
+        else:
+            norm[...] = partial[bit] + other[bit]
+
+
+def scatter_all(cube, grads, groups):
+    count = len(grads)
+    devices = 1 << cube.bits
+    shapes = [(g.shape[0] // devices, g.shape[1]) for g in grads]
+    pieces = cut_pieces(cube, [g.shape[1] for g in grads], groups)
+    scratch = [
+        pltpu.VMEM((2,) * (cube.bits - 1) + shape, g.dtype) for shape, g in zip(shapes, grads)
+    ]
+    for stage in range(cube.bits):
+        scratch += [
+            pltpu.VMEM((2,) * (cube.bits - 1 - stage) + shape, g.dtype)
+            for shape, g in zip(shapes, grads)
+        ]
+    return pl.pallas_call(
+        functools.partial(scatter_kernel, cube, pieces, count),
+        out_shape=[jax.ShapeDtypeStruct(shape, jnp.float32) for shape in shapes + [(8, 128)]],
+        in_specs=[pl.BlockSpec(memory_space=pl.ANY)] * count,
+        out_specs=[pl.BlockSpec(memory_space=pltpu.VMEM)] * (count + 1),
+        scratch_shapes=scratch
+        + [
+            pltpu.SemaphoreType.DMA((len(pieces),)),
+            pltpu.SemaphoreType.DMA((len(pieces), cube.bits)),
+            pltpu.SemaphoreType.DMA((len(pieces), cube.bits)),
+            pltpu.VMEM((cube.bits, 8, 128), jnp.float32),
+            pltpu.VMEM((cube.bits, 8, 128), jnp.float32),
+            pltpu.SemaphoreType.DMA((cube.bits,)),
+            pltpu.SemaphoreType.DMA((cube.bits,)),
+        ],
+        compiler_params=pltpu.CompilerParams(
+            collective_id=1, has_side_effects=True, vmem_limit_bytes=VMEM_BYTES
+        ),
+    )(*[g.reshape((2,) * cube.bits + s) for g, s in zip(grads, shapes)])
+
+
+GROUPS = (
+    ((0, (0, 0, 1, 0)),),
+    ((0, (2, 2, 4, 4)), (1, (2, 2, 4, 4))),
+    ((2, (0, 0, 1, 1)),),
+    ((2, (1, 1, 3, 3)),),
+    ((3, (2, 2, 4, 4)), (4, (2, 2, 4, 4)), (5, (2, 2, 4, 4)), (6, (2, 2, 4, 4))),
+    ((7, (1, 1, 1, 1)), (8, (1, 1, 1, 1))),
+)
+AXES = ("dp", "fsdp")
+
+
+def pack_vectors(temporal, scales):
+    upper = jnp.concatenate([temporal.T, jnp.pad(scales.T, ((0, 6), (0, 0)))], axis=1)
+    return jnp.pad(upper, ((0, 0), (0, 128 - upper.shape[1])))
+
+
+def gather_params(cube, misc, matrices):
+    if all(m.shape[0] % 16 == 0 for m in matrices):
+        kinds = [jnp.float32] + [BRAIN] * len(matrices)
+        return gather_all(cube, [misc] + list(matrices), kinds, GROUPS)
+    sent = [misc] + [m.astype(BRAIN) for m in matrices]
+    return [lax.all_gather(v, AXES, axis=0, tiled=True) for v in sent]
+
+
+def scatter_grads(cube, misc, grads):
+    if all((g.shape[0] >> cube.bits) % 16 == 0 for g in grads):
+        outs = scatter_all(cube, [misc] + list(grads), GROUPS)
+        return outs[:-1], outs[-1]
+    sums = [
+        lax.psum_scatter(g.astype(jnp.float32), AXES, scatter_dimension=0, tiled=True)
+        for g in [misc] + list(grads)
+    ]
+    squares = lax.psum(sum(jnp.sum(s * s) for s in sums), AXES)
+    return sums, jnp.pad(squares[None, None], ((0, 7), (0, 127)))
+
+
+def adam_kernel(count, norm_tile, *refs):
+    grads, olds, ones, twos = (refs[i * count : (i + 1) * count] for i in range(4))
+    norm_ref = refs[4 * count]
+    afters, new_ones, new_twos = (
+        refs[4 * count + 1 + i * count : 4 * count + 1 + (i + 1) * count] for i in range(3)
+    )
+    grad_norm = jnp.sqrt(jnp.sum(norm_tile[...], keepdims=True))
+    norm_ref[...] = grad_norm
+    factor = CLIP_NORM / jnp.maximum(grad_norm, CLIP_NORM)
+    for i in range(count):
+        matrix = i < count - 2
+        after, one, two = adam_update(
+            olds[i][...],
+            ones[i][...],
+            twos[i][...],
+            grads[i][...],
+            factor,
+            RATE_MATRIX if matrix else RATE_VECTOR,
+            WEIGHT_DECAY if matrix else 0.0,
+        )
+        afters[i][...] = after
+        new_ones[i][...] = one
+        new_twos[i][...] = two
+
+
+def adam_all(norm_tile, grads, olds, ones, twos):
+    count = len(grads)
+    like = [jax.ShapeDtypeStruct(v.shape, v.dtype) for v in olds]
+    return pl.pallas_call(
+        functools.partial(adam_kernel, count),
+        out_shape=[jax.ShapeDtypeStruct((1, 1), jnp.float32)] + like * 3,
+        compiler_params=pltpu.CompilerParams(vmem_limit_bytes=VMEM_BYTES),
+    )(norm_tile, *grads, *olds, *ones, *twos)
 
 
 def rms_scale(values, weights):
@@ -95,6 +444,7 @@
 
 
 def shards(
+    cube,
     tokens,
     cotangent,
     doc_lengths,
@@ -121,17 +471,14 @@
     temporal_square,
 ):
     brain = jnp.bfloat16
-    expand_full, contract_full, gating_full, scales_full, temporal_full = (
-        lax.all_gather(expand.astype(brain), ("dp", "fsdp"), axis=0, tiled=True),
-        lax.all_gather(contract.astype(brain), ("dp", "fsdp"), axis=0, tiled=True),
-        lax.all_gather(gating.astype(brain), ("dp", "fsdp"), axis=0, tiled=True),
-        lax.all_gather(scales.astype(brain), ("dp", "fsdp"), axis=0, tiled=True),
-        lax.all_gather(temporal.astype(brain), ("dp", "fsdp"), axis=0, tiled=True),
-    )
-    widen_full, narrow_full = (
-        lax.all_gather(widen.astype(brain), ("dp", "fsdp"), axis=0, tiled=True),
-        lax.all_gather(narrow.astype(brain), ("dp", "fsdp"), axis=0, tiled=True),
-    )
+    rows_t, rows_s = temporal.shape[0], scales.shape[0]
+    vectors = pack_vectors(temporal, scales).astype(brain).astype(jnp.float32)
+    vectors, expand_full, gating_full, contract_full, widen_full, narrow_full = gather_params(
+        cube, vectors, (expand, gating, contract, widen, narrow)
+    )
+    vectors = vectors.reshape(-1, 8, 128).transpose(0, 2, 1)
+    temporal_float = vectors[:, :rows_t].reshape(-1, 8)
+    scales_float = vectors[:, rows_t : rows_t + rows_s, :2].reshape(-1, 2)
     width = contract_full.shape[0]
     hidden = narrow_full.shape[0]
     head_width = gating_full.shape[1] // 2
@@ -141,8 +488,6 @@
     resets = resets[0]
     segment = segment[0]
     inputs = tokens[0].astype(jnp.float32)
-    scales_float = scales_full.astype(jnp.float32)
-    temporal_float = temporal_full.astype(jnp.float32)
     normed, norm_pull = jax.vjp(rms_scale, inputs, scales_float[:, 0])
     normed_low = normed.astype(brain)
     projected = jnp.dot(normed_low, expand_full, preferred_element_type=jnp.float32)
@@ -186,10 +531,6 @@
     block_out = (
         middle + jnp.dot(activated_low, narrow_full, preferred_element_type=jnp.float32)
     ).astype(brain)
-    widen_full, narrow_full = (
-        lax.all_gather(widen.astype(brain), ("dp", "fsdp"), axis=0, tiled=True),
-        lax.all_gather(narrow.astype(brain), ("dp", "fsdp"), axis=0, tiled=True),
-    )
     upstream = cotangent[0]
     narrow_grad = product_rows(activated_low, upstream)
     activated_grad = product_cols(upstream, narrow_full)
@@ -198,11 +539,6 @@
     normed_two_grad = product_cols(widened_grad, widen_full)
     middle_norm_grad, scale_two_grad = norm_two_pull(normed_two_grad)
     middle_grad = upstream.astype(jnp.float32) + middle_norm_grad
-    expand_full, contract_full, gating_full = (
-        lax.all_gather(expand.astype(brain), ("dp", "fsdp"), axis=0, tiled=True),
-        lax.all_gather(contract.astype(brain), ("dp", "fsdp"), axis=0, tiled=True),
-        lax.all_gather(gating.astype(brain), ("dp", "fsdp"), axis=0, tiled=True),
-    )
     middle_low = middle_grad.astype(brain)
     contract_grad = product_rows(mixed_low, middle_low)
     mixed_grad = product_cols(middle_low, contract_full)
@@ -223,71 +559,37 @@
     tokens_grad = (middle_grad + token_norm_grad).astype(brain)
     scales_grad = jnp.stack([scale_one_grad, scale_two_grad], axis=1)
     temporal_grad = jnp.concatenate([taps_grad, conv_bias_grad[:, None], recur_bias_grad], axis=1)
-    summed = (
-        lax.psum_scatter(expand_grad, ("dp", "fsdp"), scatter_dimension=0, tiled=True),
-        lax.psum_scatter(contract_grad, ("dp", "fsdp"), scatter_dimension=0, tiled=True),
-        lax.psum_scatter(gating_grad, ("dp", "fsdp"), scatter_dimension=0, tiled=True),
-        lax.psum_scatter(widen_grad, ("dp", "fsdp"), scatter_dimension=0, tiled=True),
-        lax.psum_scatter(narrow_grad, ("dp", "fsdp"), scatter_dimension=0, tiled=True),
-        lax.psum_scatter(scales_grad, ("dp", "fsdp"), scatter_dimension=0, tiled=True),
-        lax.psum_scatter(temporal_grad, ("dp", "fsdp"), scatter_dimension=0, tiled=True),
-    )
-    local_squares = jnp.float32(0.0)
-    for piece in summed:
-        local_squares = local_squares + jnp.sum(piece * piece)
-    grad_norm = jnp.sqrt(lax.psum(local_squares, ("dp", "fsdp")))
-    factor = CLIP_NORM / jnp.maximum(grad_norm, CLIP_NORM)
-    masters = (expand, contract, gating, widen, narrow, scales, temporal)
-    moments = (
-        (expand_mean, expand_square),
-        (contract_mean, contract_square),
-        (gating_mean, gating_square),
-        (widen_mean, widen_square),
-        (narrow_mean, narrow_square),
-        (scales_mean, scales_square),
-        (temporal_mean, temporal_square),
-    )
-    updated = []
-    for index in range(7):
-        rate = RATE_MATRIX if index < 5 else RATE_VECTOR
-        decay = WEIGHT_DECAY if index < 5 else 0.0
-        updated.append(
-            adam_update(
-                masters[index],
-                moments[index][0],
-                moments[index][1],
-                summed[index],
-                factor,
-                rate,
-                decay,
-            )
-        )
-    return (
-        block_out[None],
-        tokens_grad[None],
-        grad_norm,
-        updated[0][0],
-        updated[0][1],
-        updated[0][2],
-        updated[1][0],
-        updated[1][1],
-        updated[1][2],
-        updated[2][0],
-        updated[2][1],
-        updated[2][2],
-        updated[3][0],
-        updated[3][1],
-        updated[3][2],
-        updated[4][0],
-        updated[4][1],
-        updated[4][2],
-        updated[5][0],
-        updated[5][1],
-        updated[5][2],
-        updated[6][0],
-        updated[6][1],
-        updated[6][2],
-    )
+    devices = 1 << cube.bits
+    misc = jnp.concatenate(
+        [
+            temporal_grad.T.reshape(8, devices, rows_t),
+            jnp.pad(scales_grad.T, ((0, 6), (0, 0))).reshape(8, devices, rows_s),
+        ],
+        axis=2,
+    )
+    misc = jnp.pad(misc, ((0, 0), (0, 0), (0, 128 - rows_t - rows_s)))
+    misc = misc.transpose(1, 0, 2).reshape(devices * 8, 128)
+    matrices = (expand_grad, gating_grad, contract_grad, widen_grad, narrow_grad)
+    sums, norm_tile = scatter_grads(cube, misc, [g.astype(brain) for g in matrices])
+    grads = list(sums[1:]) + [sums[0][:2, rows_t : rows_t + rows_s].T, sums[0][:, :rows_t].T]
+    outs = adam_all(
+        norm_tile,
+        grads,
+        (expand, gating, contract, widen, narrow, scales, temporal),
+        (expand_mean, gating_mean, contract_mean, widen_mean, narrow_mean, scales_mean, temporal_mean),
+        (
+            expand_square,
+            gating_square,
+            contract_square,
+            widen_square,
+            narrow_square,
+            scales_square,
+            temporal_square,
+        ),
+    )
+    grad_norm, outs = outs[0][0, 0], outs[1:]
+    updated = [outs[i + 7 * j] for i in (0, 2, 1, 3, 4, 5, 6) for j in range(3)]
+    return (block_out[None], tokens_grad[None], grad_norm, *updated)
 
 
 def solution(mesh):
@@ -318,7 +620,7 @@
         P(("dp", "fsdp"), None),
     )
     return jax.shard_map(
-        shards,
+        functools.partial(shards, Cube(mesh.shape)),
         mesh=mesh,
         in_specs=placed,
         out_specs=(

time: 2050 us -> 917 us (0.45)
  waiting for transfers between devices: 953 us -> 0 us
  Pallas kernels: 0 us -> 287 us
  blocking collectives: 253 us -> 0 us
  local copies, waits for them, and re-layouts: 457 us -> 357 us
  other arithmetic: 210 us -> 147 us
    reduce_scatter x5 -> x0, waiting for transfers between devices: 786 us -> none  [the longest x1 249 us: shards(): lax.psum_scatter(widen_grad, ('dp', 'fsdp'), scatter_dimension=0, tiled=T...]
    pallas_call x0 -> x3, Pallas kernels: none -> 287 us  [the longest x1 146 us: scatter_all(): pl.pallas_call(functools.partial(scatter_kernel, cube, pieces, count), ou...]
    all_gather x3 -> x0, blocking collectives: 213 us -> none  [the longest x1 79.1 us: shards(): lax.all_gather(gating.astype(brain), ('dp', 'fsdp'), axis=0, tiled=True)]
    unnamed x13 -> x0, waiting for transfers between devices: 167 us -> none
    pad x70, local copies, waits for them, and re-layouts: 234 us -> 169 us  [recurrence(): return lax.associative_scan(combine_linear, (decays, inputs), axis=-2)[1]]
    slice x69, local copies, waits for them, and re-layouts: 180 us -> 131 us  [recurrence(): return lax.associative_scan(combine_linear, (decays, inputs), axis=-2)[1]]
    psum x1 -> x0, blocking collectives: 40.1 us -> none  [shards(): grad_norm = jnp.sqrt(lax.psum(local_squares, ('dp', 'fsdp')))]
  transfers between devices with their start and end apart: 11 -> 0, of which waited for: 7 -> 0; matrix products, arithmetic and copies ran while one was open for 19% -> 0% of each run, Pallas kernels for 0% -> 0%
where the time goes in v1:
time: 917 us; the launch traced here: 907 us
  local copies, waits for them, and re-layouts  357 us (39%)
  Pallas kernels  287 us (31%)
  other arithmetic  147 us (16%)
  matrix products  113 us (12%)
    pad x70, local copies, waits for them, and re-layouts, recurrence(): return lax.associative_scan(combine_linear, (decays, inputs), axis=-2)[1]  169 us
    pallas_call x1, Pallas kernels, scatter_all(): pl.pallas_call(functools.partial(scatter_kernel, cube, pieces, count), ou...  146 us
    pallas_call x1, Pallas kernels, gather_all(): pl.pallas_call(functools.partial(gather_kernel, cube, pieces, count), out...  134 us
    slice x69, local copies, waits for them, and re-layouts, recurrence(): return lax.associative_scan(combine_linear, (decays, inputs), axis=-2)[1]  131 us
    dot_general x4, matrix products, product_cols(): lax.dot_general(former, latter, (((1,), (1,)), ((), ())), preferred_eleme...  41.2 us
    dot_general x4, matrix products, product_rows(): lax.dot_general(former, latter, (((0,), (0,)), ((), ())), preferred_eleme...  33 us
    unnamed x318, local copies, waits for them, and re-layouts  26.9 us
    mul x15, other arithmetic, combine_linear(): return (earlier[0] * later[0], later[0] * earlier[1] + later[1])  23 us

profile of v1, /device:TPU:0, one launch (start us, length us, event | category | flops | bytes accessed | tf_op | source)
XLA Modules:
  0.0 906.6 jit_solution(12030281610772417693)
XLA Ops:
  2.8 134.1 %shard_map.415 = (f32[2,2,2,2,2,8,128]{6,5,4,3,2,1,0:T(8,128)}, bf16[2,2,2,2,2,32,3072]{6,5,4,3,2,1,0:T(8,128)(2,1)}, bf16[2,2,2,2,2,48,256]{6,5,4,3,2,1,0:T(8,1...) custom-call(f32[8,128]{1,0:T(8,128)} %pad_convert_fusion.refs_0_, ...), custom_call_target="tpu_custom_call" | custom-call | tf_op jit(solution)/shard_map/pallas_call | solution.py:137
  139.6 8.8 fusion.37
  173.7 7.5 exponential_multiply_fusion
  181.2 7.4 slice.459
  197.3 6.1 slice.395
  203.5 7.3 slice.397
  210.7 7.1 slice.396
  336.0 9.6 %pad.415 = f32[512,1536]{1,0:T(8,128)} pad(f32[256,1536]{1,0:T(8,128)} %pad_maximum_fusion.3, f32[]{:T(128)} %constant.21.clone.1), padding=0_1_1x0_0_0 | pad | bytes 4718596 | tf_op jit(solution)/shard_map/jvp()/pad | solution.py:406
  348.5 9.8 %pad.416 = f32[512,1536]{1,0:T(8,128)} pad(f32[256,1536]{1,0:T(8,128)} %add.448, f32[]{:T(128)} %constant.21.clone.1), padding=1_0_1x0_0_0 | pad | bytes 4718596 | tf_op jit(solution)/shard_map/jvp()/pad | solution.py:406
  358.2 6.8 multiply_convert_fusion.1
  369.3 9.3 %fusion.89 = f32[512,6144]{1,0:T(8,128)} fusion(bf16[1024,6144]{1,0:T(8,128)(2,1)S(1)} %bitcast.167, f32[512,1024]{1,0:T(8,128)S(1)} %get-tuple-element.311, f32[1024]{0:T(1024)S(1)} %bitcast.148, f32[512]{0:T(512)S(1)} %fusion.73), kind=kOutput, calls=%fused_computation.256 | convolution fusion | flops 6444023808 | bytes 27269120 | tf_op jit(solution)/shard_map/dot_general | solution.py:524
  378.6 15.3 %bitcast_multiply_fusion.1 = (f32[512,3072]{1,0:T(8,128)}, f32[512,3072]{1,0:T(8,128)}, bf16[512,3072]{1,0:T(8,128)(2,1)S(1)}) fusion(f32[512,6144]{1,0:T(8,128)} %fusion.89, bf16[3072,1024]{1,0:T(8,128)(2,1)} %bitcast.172, bf16[1,512,1024]{2,1,0:T(8,128)(2,1)S(1)} %copy-done.65), kind=kOutput, calls=%fused_computation.11 | convolution fusion | flops 3258974208 | bytes 35651584 | tf_op jit(solution)/shard_map/dot_general | solution.py:431
  393.9 8.4 fusion.33
  402.3 15.5 %multiply_reduce_fusion.5 = (f32[1024]{0:T(1024)}, f32[512]{0:T(512)S(1)}, f32[512,1024]{1,0:T(8,128)}) fusion(f32[512,1024]{1,0:T(8,128)} %copy-done.24, f32[512]{0:T(512)S(1)} %fusion.73, f32[1024]{0:T(1024)S(1)} %bitcast.149, bf16[1024,6144]{1,0:T(8,128)(2,1)} %bitcast.164, f32[512,3072]{1,0:T(8,128)} %get-tuple-element.213, ...), kind=kOutput, calls=%fused_computation.75 | convolution fusion | flops 6451886592 | bytes 29372416 | tf_op jit(solution)/shard_map/dot_general | solution.py:431
  422.7 6.6 fusion.34
  432.5 7.1 slice.465
  439.7 7.1 slice.464
  593.3 6.1 multiply_add_fusion.3
  599.4 9.7 %pad.504 = f32[512,1536]{1,0:T(8,128)} pad(f32[256,1536]{1,0:T(8,128)} %get-tuple-element.220, f32[]{:T(128)} %constant.21.clone.1), padding=0_1_1x0_0_0 | pad | bytes 4718596 | tf_op jit(solution)/shard_map/transpose(jvp())/pad | solution.py:406
  609.1 5.8 pad.480
  615.0 9.7 %pad.503 = f32[512,1536]{1,0:T(8,128)} pad(f32[256,1536]{1,0:T(8,128)} %get-tuple-element.219, f32[]{:T(128)} %constant.21.clone.1), padding=1_0_1x0_0_0 | pad | bytes 4718596 | tf_op jit(solution)/shard_map/transpose(jvp())/pad | solution.py:406
  624.7 5.8 pad.478
  630.5 5.8 pad.477
  636.3 10.3 %pad.421 = f32[512,1536]{1,0:T(8,128)} pad(f32[255,1536]{1,0:T(8,128)} %get-tuple-element.232, f32[]{:T(128)} %constant.21.clone.1), padding=2_1_1x0_0_0 | pad | bytes 4712452 | tf_op jit(solution)/shard_map/transpose(jvp())/pad | solution.py:406
  646.7 10.7 %multiply_reduce_fusion = (f32[1536]{0:T(1024)S(1)}, f32[512,1536]{1,0:T(8,128)S(1)}, f32[512,1536]{1,0:T(8,128)S(1)}) fusion(f32[512,1536]{1,0:T(8,128)S(1)} %copy-done.1, f32[1536]{0:T(1024)S(1)} %copy-done.94, f32[512,1536]{1,0:T(8,128)} %pad.504, f32[512,1536]{1,0:T(8,128)} %pad.480, f32[512,1536]{1,0:T(8,128)} %pad.503, f32[1536]{0:T(1024)S(1)} %copy-done.98, ...), kind=kLoop, calls=%fused_computation.37 | loop fusion | flops 24377856 | bytes 33062912 | tf_op jit(solution)/shard_map/transpose(jvp())/reduce_sum | solution.py:416
  657.4 6.5 fusion.90
  679.9 7.8 multiply_reduce_fusion.4
  702.8 7.4 convolution_convert_fusion.2
  716.0 14.6 %convolution_convert_fusion = bf16[1024,6144]{1,0:T(8,128)(2,1)} fusion(f32[512,3072]{1,0:T(8,128)} %get-tuple-element.213, f32[512,3072]{1,0:T(8,128)} %get-tuple-element.212, f32[512,1024]{1,0:T(8,128)S(1)} %copy-done.25, f32[1024]{0:T(1024)S(1)} %bitcast.151, f32[512]{0:T(512)S(1)} %copy-done.92), kind=kOutput, calls=%fused_computation.1 | convolution fusion | flops 6456606720 | bytes 27269120 | tf_op jit(solution)/shard_map/dot_general | solution.py:425
  730.6 7.3 convolution_convert_fusion.1
  738.0 146.3 %shard_map.416 = (f32[8,128]{1,0:T(8,128)}, f32[32,3072]{1,0:T(8,128)}, f32[48,256]{1,0:T(8,128)}, f32[48,1024]{1,0:T(8,128)}, f32[32,6144]{1,0:T(8,128)}, /*index=5*/f32[96,1024]{1,0:T(8,128)}, f32[8,128]{1,0:T(8,128)}) custom-call(f32[2,2,2,2,2,8,128]{6,5,4,3,2,1,0:T(8,128)} %bitcast.147, bf16[2,2,2,2,2,32,3072]{6,5,4,3,2,1,0:T(8,128)(2,1)} %bitcast.139, ...), custom_call_target="tpu_custom_call" | custom-call | tf_op jit(solution)/shard_map/pallas_call | solution.py:277
  891.2 7.0 shard_map.417
  (589 shorter events, 368.9 us)
Async XLA Ops:
  0.7 138.9 %copy-start.39 = (bf16[1,512,1024]{2,1,0:T(8,128)(2,1)S(1)}, bf16[1,512,1024]{2,1,0:T(8,128)(2,1)}, u32[]{:S(2)}) copy-start(bf16[1,512,1024]{2,1,0:T(8,128)(2,1)} %param.24) | copy-start | bytes 3145732
  138.0 279.7 %copy-start.80 = (f32[1024,1]{0,1:T(1,128)}, f32[1024,1]{0,1:T(1,128)S(1)}, u32[]{:S(2)}) copy-start(f32[1024,1]{0,1:T(1,128)S(1)} %get-tuple-element.305) | copy-start | bytes 12292
  148.7 25.0 %copy-start.117 = (f32[512]{0:T(512)}, f32[512]{0:T(512)S(1)}, u32[]{:S(2)}) copy-start(f32[512]{0:T(512)S(1)} %broadcast_subtract_fusion) | copy-start | bytes 6148
  149.0 24.7 %copy-start.93 = (f32[1536]{0:T(1024)}, f32[1536]{0:T(1024)S(1)}, u32[]{:S(2)}) copy-start(f32[1536]{0:T(1024)S(1)} %get-tuple-element.172) | copy-start | bytes 18436
  149.0 24.7 %copy-start.95 = (f32[1536]{0:T(1024)}, f32[1536]{0:T(1024)S(1)}, u32[]{:S(2)}) copy-start(f32[1536]{0:T(1024)S(1)} %get-tuple-element.173) | copy-start | bytes 18436
  149.6 24.1 %copy-start.97 = (f32[1536]{0:T(1024)}, f32[1536]{0:T(1024)S(1)}, u32[]{:S(2)}) copy-start(f32[1536]{0:T(1024)S(1)} %get-tuple-element.304) | copy-start | bytes 18436
  203.5 14.4 %copy-start.15 = (f32[256,1536]{1,0:T(8,128)S(1)}, f32[256,1536]{1,0:T(8,128)}, u32[]{:S(2)}) copy-start(f32[256,1536]{1,0:T(8,128)} %slice.399) | copy-start | bytes 4718596
  225.1 15.0 %copy-start.29 = (f32[128,1536]{1,0:T(8,128)}, f32[128,1536]{1,0:T(8,128)S(1)}, u32[]{:S(2)}) copy-start(f32[128,1536]{1,0:T(8,128)S(1)} %slice.405) | copy-start | bytes 2359300
  228.5 11.6 %copy-start.18 = (f32[128,1536]{1,0:T(8,128)}, f32[128,1536]{1,0:T(8,128)S(1)}, u32[]{:S(2)}) copy-start(f32[128,1536]{1,0:T(8,128)S(1)} %slice.401) | copy-start | bytes 2359300
  247.7 12.9 %copy-start.42 = (f32[64,1536]{1,0:T(8,128)}, f32[64,1536]{1,0:T(8,128)S(1)}, u32[]{:S(2)}) copy-start(f32[64,1536]{1,0:T(8,128)S(1)} %slice.411) | copy-start | bytes 1179652
  251.7 18.1 %copy-start.43 = (f32[64,1536]{1,0:T(8,128)}, f32[64,1536]{1,0:T(8,128)S(1)}, u32[]{:S(2)}) copy-start(f32[64,1536]{1,0:T(8,128)S(1)} %slice.408) | copy-start | bytes 1179652
  265.2 29.5 %copy-start.70 = (f32[15,1536]{1,0:T(8,128)}, f32[15,1536]{1,0:T(8,128)S(1)}, u32[]{:S(2)}) copy-start(f32[15,1536]{1,0:T(8,128)S(1)} %slice.418) | copy-start | bytes 276484
  266.2 28.5 %copy-start.67 = (f32[16,1536]{1,0:T(8,128)}, f32[16,1536]{1,0:T(8,128)S(1)}, u32[]{:S(2)}) copy-start(f32[16,1536]{1,0:T(8,128)S(1)} %slice.423) | copy-start | bytes 294916
  267.2 27.5 %copy-start.58 = (f32[16,1536]{1,0:T(8,128)}, f32[16,1536]{1,0:T(8,128)S(1)}, u32[]{:S(2)}) copy-start(f32[16,1536]{1,0:T(8,128)S(1)} %slice.419) | copy-start | bytes 294916
  269.8 24.9 %copy-start.68 = (f32[16,1536]{1,0:T(8,128)}, f32[16,1536]{1,0:T(8,128)S(1)}, u32[]{:S(2)}) copy-start(f32[16,1536]{1,0:T(8,128)S(1)} %slice.420) | copy-start | bytes 294916
  272.3 19.1 %copy-start.76 = (f32[8,1536]{1,0:T(8,128)}, f32[8,1536]{1,0:T(8,128)S(1)}, u32[]{:S(2)}) copy-start(f32[8,1536]{1,0:T(8,128)S(1)} %slice.429) | copy-start | bytes 147460
  273.3 18.1 %copy-start.72 = (f32[8,1536]{1,0:T(8,128)}, f32[8,1536]{1,0:T(8,128)S(1)}, u32[]{:S(2)}) copy-start(f32[8,1536]{1,0:T(8,128)S(1)} %slice.425) | copy-start | bytes 147460
  275.1 16.3 %copy-start.77 = (f32[8,1536]{1,0:T(8,128)}, f32[8,1536]{1,0:T(8,128)S(1)}, u32[]{:S(2)}) copy-start(f32[8,1536]{1,0:T(8,128)S(1)} %slice.426) | copy-start | bytes 147460
  277.6 25.1 %copy-start.104 = (f32[1,1536]{1,0:T(1,128)}, f32[1,1536]{1,0:T(1,128)S(1)}, u32[]{:S(2)}) copy-start(f32[1,1536]{1,0:T(1,128)S(1)} %get-tuple-element.301) | copy-start | bytes 18436
  367.0 26.9 %copy-start.24 = (f32[512,1024]{1,0:T(8,128)}, f32[512,1024]{1,0:T(8,128)S(1)}, u32[]{:S(2)}) copy-start(f32[512,1024]{1,0:T(8,128)S(1)} %get-tuple-element.311) | copy-start | bytes 6291460
  369.3 48.5 %copy-start.91 = (f32[512]{0:T(512)}, f32[512]{0:T(512)S(1)}, u32[]{:S(2)}) copy-start(f32[512]{0:T(512)S(1)} %fusion.73) | copy-start | bytes 6148
  483.2 12.7 %slice-start.5 = ((f32[32,1536]{1,0:T(8,128)}), f32[1,1536]{1,0:T(1,128)S(1)}, s32[]{:S(2)}) async-start(f32[32,1536]{1,0:T(8,128)} %copy-done.71), calls=%async_computation.5 | async-start | bytes 12288 | tf_op jit(solution)/shard_map/transpose(jvp())/split | solution.py:406
  490.4 12.5 %copy-start.60 = (f32[63,1536]{1,0:T(8,128)S(1)}, f32[63,1536]{1,0:T(8,128)}, u32[]{:S(2)}) copy-start(f32[63,1536]{1,0:T(8,128)} %get-tuple-element.250) | copy-start | bytes 1161220
  507.5 11.6 %copy-start.30 = (f32[128,1536]{1,0:T(8,128)}, f32[128,1536]{1,0:T(8,128)S(1)}, u32[]{:S(2)}) copy-start(f32[128,1536]{1,0:T(8,128)S(1)} %get-tuple-element.197) | copy-start | bytes 2359300
  507.5 11.6 %slice-start.3 = ((f32[128,1536]{1,0:T(8,128)}), f32[1,1536]{1,0:T(1,128)S(1)}, s32[]{:S(2)}) async-start(f32[128,1536]{1,0:T(8,128)} %slice.466), calls=%async_computation.3 | async-start | bytes 12288 | tf_op jit(solution)/shard_map/transpose(jvp())/split | solution.py:406
  716.0 14.6 %copy-start.66 = (bf16[1,512,1024]{2,1,0:T(8,128)(2,1)S(1)}, bf16[1,512,1024]{2,1,0:T(8,128)(2,1)}, u32[]{:S(2)}) copy-start(bf16[1,512,1024]{2,1,0:T(8,128)(2,1)} %param.25) | copy-start | bytes 3145732
  737.9 149.1 %copy-start.138 = (f32[32,2]{0,1:T(2,128)S(1)}, f32[32,2]{0,1:T(2,128)}, u32[]{:S(2)}) copy-start(f32[32,2]{0,1:T(2,128)} %param.42) | copy-start | bytes 772
  737.9 149.8 %copy-start.132 = (f32[48,8]{0,1:T(8,128)S(1)}, f32[48,8]{0,1:T(8,128)}, u32[]{:S(2)}) copy-start(f32[48,8]{0,1:T(8,128)} %param.45) | copy-start | bytes 4612
  737.9 150.5 %copy-start.139 = (f32[32,2]{0,1:T(2,128)S(1)}, f32[32,2]{0,1:T(2,128)}, u32[]{:S(2)}) copy-start(f32[32,2]{0,1:T(2,128)} %param.43) | copy-start | bytes 772
  737.9 151.2 %copy-start.135 = (f32[48,8]{0,1:T(8,128)S(1)}, f32[48,8]{0,1:T(8,128)}, u32[]{:S(2)}) copy-start(f32[48,8]{0,1:T(8,128)} %param.46) | copy-start | bytes 4612
  738.0 151.9 %copy-start.140 = (f32[32,2]{0,1:T(2,128)S(1)}, f32[32,2]{0,1:T(2,128)}, u32[]{:S(2)}) copy-start(f32[32,2]{0,1:T(2,128)} %param.44) | copy-start | bytes 772
  738.0 152.5 %copy-start.136 = (f32[48,8]{0,1:T(8,128)S(1)}, f32[48,8]{0,1:T(8,128)}, u32[]{:S(2)}) copy-start(f32[48,8]{0,1:T(8,128)} %param.47) | copy-start | bytes 4612
  (125 other events, 725.7 us)

commit v2 on v1

--- a/solution.py
+++ b/solution.py
@@ -366,59 +366,365 @@
     )(norm_tile, *grads, *olds, *ones, *twos)
 
 
-def rms_scale(values, weights):
-    return (
-        values
-        * lax.rsqrt(jnp.mean(values * values, axis=-1, keepdims=True) + NORM_EPSILON)
-        * weights
-    )
-
-
-def doc_tables(lengths, length):
-    starts = jnp.cumsum(lengths, axis=-1) - lengths
+GELU_ONE = 0.7978845608028654
+GELU_THREE = GELU_ONE * 0.044715
+LANES = 128
+ROWS = 8
+
+
+def sigmoid(v):
+    return 0.5 * jnp.tanh(0.5 * v) + 0.5
+
+
+def gelu_parts(v):
+    square = v * v
+    turned = jnp.tanh(v * (GELU_ONE + GELU_THREE * square))
+    half = 0.5 * turned + 0.5
+    slope = half + (0.5 * v) * (1.0 - turned * turned) * (GELU_ONE + (3.0 * GELU_THREE) * square)
+    return half, slope
+
+
+def gelu_half(v):
+    return 0.5 * jnp.tanh(v * (GELU_ONE + GELU_THREE * (v * v))) + 0.5
+
+
+def one_less_exp(v, exp_v):
+    series = 1.0 + v * (1.0 / 7.0)
+    for order in (6.0, 5.0, 4.0, 3.0, 2.0):
+        series = 1.0 + v * (1.0 / order) * series
+    return jnp.where(v > -0.35, -v * series, 1.0 - exp_v)
+
+
+def row_mask(width, first, last):
+    rows = lax.broadcasted_iota(jnp.int32, (ROWS, width), 0)
+    return (rows >= first) & (rows < last)
+
+
+def shifted_down(now, before, steps, mask):
+    return jnp.where(mask, pltpu.roll(now, steps, 0), pltpu.roll(before, steps, 0))
+
+
+def shifted_up(now, after, steps, mask):
+    return jnp.where(mask, pltpu.roll(now, ROWS - steps, 0), pltpu.roll(after, ROWS - steps, 0))
+
+
+def wide(column, width):
+    return column if width == LANES else jnp.concatenate([column] * (width // LANES), axis=1)
+
+
+def rms_rows(source, gain, target, places):
+    def one(tile, carry):
+        rows = pl.ds(pl.multiple_of(tile * 16, 16), 16)
+        v = source[rows, :].astype(jnp.float32)
+        scale = lax.rsqrt(jnp.mean(v * v, axis=-1, keepdims=True) + NORM_EPSILON)
+        target[rows, :] = (v * scale * gain[...]).astype(target.dtype)
+        return carry
+
+    lax.fori_loop(0, places // 16, one, 0, unroll=2)
+
+
+def conv_forward(u, vec, masks, conv, lanes, width, places):
+    taps = [jnp.broadcast_to(vec[k : k + 1, lanes], (ROWS, width)) for k in range(5)]
+    inside = [row_mask(width, k, ROWS) for k in range(4)]
+
+    def one(tile, before):
+        parts = []
+        for half in range(2):
+            rows = pl.ds(pl.multiple_of(tile * 16 + half * 8, 8), ROWS)
+            now = u[rows, lanes]
+            total = taps[4] + now * taps[0]
+            for k in range(1, 4):
+                keep = wide(masks[k - 1, rows, :], width)
+                total = total + shifted_down(now, before, k, inside[k]) * taps[k] * keep
+            parts.append(total)
+            before = now
+        rows = pl.ds(pl.multiple_of(tile * 16, 16), 16)
+        conv[rows, lanes] = jnp.concatenate(parts, axis=0).astype(conv.dtype)
+        return before
+
+    lax.fori_loop(0, places // 16, one, jnp.zeros((ROWS, width), jnp.float32), unroll=2)
+
+
+def scan_tile(decay, value, masks, sign):
+    for steps, mask in zip((1, 2, 4), masks):
+        turn = steps if sign > 0 else ROWS - steps
+        value = value + decay * jnp.where(mask, pltpu.roll(value, turn, 0), 0.0)
+        decay = decay * jnp.where(mask, pltpu.roll(decay, turn, 0), 1.0)
+    return decay, value
+
+
+def mix_forward(recur, inlet, branch, conv, vec, masks, state, mixed, lanes, width, places):
+    bias_r = jnp.broadcast_to(vec[5:6, lanes], (ROWS, width))
+    bias_i = jnp.broadcast_to(vec[6:7, lanes], (ROWS, width))
+    power = jnp.broadcast_to(vec[8:9, lanes], (ROWS, width))
+    inside = [row_mask(width, k, ROWS) for k in (1, 2, 4)]
+
+    def one(tile, carry):
+        low_rows = pl.ds(pl.multiple_of(tile * 16, 16), 16)
+        convs = conv[low_rows, lanes].astype(jnp.float32)
+        parts = []
+        for half in range(2):
+            rows = pl.ds(pl.multiple_of(tile * 16 + half * 8, 8), ROWS)
+            going = wide(masks[0, rows, :], width)
+            gate_r = sigmoid(recur[rows, lanes] + bias_r)
+            gate_i = sigmoid(inlet[rows, lanes] + bias_i)
+            recur[rows, lanes] = gate_r
+            inlet[rows, lanes] = gate_i
+            log_decay = gate_r * power
+            decay = jnp.exp(log_decay)
+            scaling = jnp.sqrt(one_less_exp(2.0 * log_decay, decay * decay))
+            scaling = scaling * going + (1.0 - going)
+            value = scaling * gate_i * convs[half * 8 : half * 8 + 8]
+            span, value = scan_tile(decay * going, value, inside, 1)
+            value = value + span * carry
+            carry = jnp.broadcast_to(value[ROWS - 1 : ROWS, :], (ROWS, width))
+            state[rows, lanes] = value
+            gate_b = branch[rows, lanes]
+            parts.append(value * (gate_b * gelu_half(gate_b)))
+        mixed[low_rows, lanes] = jnp.concatenate(parts, axis=0).astype(mixed.dtype)
+        return carry
+
+    lax.fori_loop(0, places // 16, one, jnp.zeros((ROWS, width), jnp.float32), unroll=2)
+
+
+def mix_backward(
+    grad, recur, inlet, branch, conv, state, vec, masks, low_r, low_i, direct, low_b, tallies, lanes, width, places
+):
+    power = jnp.broadcast_to(vec[8:9, lanes], (ROWS, width))
+    below = [row_mask(width, 0, ROWS - k) for k in (1, 2, 4)]
+    first = row_mask(width, 1, ROWS)
+    tiles = places // 16
+    nothing = jnp.zeros((ROWS, width), jnp.float32)
+
+    def one(step, carries):
+        carry, after, sum_r, sum_i, sum_p = carries
+        tile = tiles - 1 - step
+        low_rows = pl.ds(pl.multiple_of(tile * 16, 16), 16)
+        convs = conv[low_rows, lanes].astype(jnp.float32)
+        outs = [[None, None] for _ in range(4)]
+        for half in (1, 0):
+            at = tile * 16 + half * 8
+            rows = pl.ds(pl.multiple_of(at, 8), ROWS)
+            going = wide(masks[0, rows, :], width)
+            gate_r, gate_i = recur[rows, lanes], inlet[rows, lanes]
+            values = convs[half * 8 : half * 8 + 8]
+            now = state[rows, lanes]
+            earlier = state[pl.ds(pl.multiple_of(jnp.maximum(at - 8, 0), 8), ROWS), lanes]
+            last = shifted_down(now, earlier, 1, first)
+            log_decay = gate_r * power
+            plain = jnp.exp(log_decay)
+            square = plain * plain
+            lost = one_less_exp(2.0 * log_decay, square)
+            inverse = lax.rsqrt(lost)
+            scaling = (lost * inverse) * going + (1.0 - going)
+            gate_b = branch[rows, lanes]
+            half_b, slope_b = gelu_parts(gate_b)
+            mixed_grad = grad[rows, lanes]
+            decay = plain * going
+            later = shifted_up(decay, after, 1, below[0])
+            span, total = scan_tile(later, mixed_grad * (gate_b * half_b), below, -1)
+            total = total + span * carry
+            carry = jnp.broadcast_to(total[0:1, :], (ROWS, width))
+            after = decay
+            outs[3][half] = mixed_grad * now * slope_b
+            scaled = total * scaling
+            flow = total * gate_i
+            outs[2][half] = scaled * gate_i
+            grad_i = scaled * values * (gate_i * (1.0 - gate_i))
+            log_grad = going * (total * last * plain - flow * values * (square * inverse))
+            grad_p = gate_r * log_grad
+            grad_r = grad_p * ((1.0 - gate_r) * power)
+            outs[0][half], outs[1][half] = grad_r, grad_i
+            sum_r, sum_i, sum_p = sum_r + grad_r, sum_i + grad_i, sum_p + grad_p
+        for target, parts in zip((low_r, low_i, direct, low_b), outs):
+            target[low_rows, lanes] = jnp.concatenate(parts, axis=0).astype(target.dtype)
+        return carry, after, sum_r, sum_i, sum_p
+
+    sums = lax.fori_loop(0, tiles, one, (nothing,) * 5, unroll=2)[2:]
+    tallies[5:6, lanes] = jnp.sum(sums[0], axis=0, keepdims=True)
+    tallies[6:7, lanes] = jnp.sum(sums[1], axis=0, keepdims=True)
+    tallies[7:8, lanes] = jnp.sum(sums[2], axis=0, keepdims=True) * vec[9:10, lanes]
+
+
+def conv_backward(direct, u, vec, masks, low_u, tallies, lanes, width, places):
+    taps = [jnp.broadcast_to(vec[k : k + 1, lanes], (ROWS, width)) for k in range(4)]
+    inside = [row_mask(width, k, ROWS) for k in range(4)]
+    below = [row_mask(width, 0, ROWS - k) for k in range(4)]
+    tiles = places // 16
+    nothing = jnp.zeros((ROWS, width), jnp.float32)
+
+    def one(step, carries):
+        afters, sums = list(carries[:3]), list(carries[3:])
+        tile = tiles - 1 - step
+        parts = [None, None]
+        for half in (1, 0):
+            at = tile * 16 + half * 8
+            rows = pl.ds(pl.multiple_of(at, 8), ROWS)
+            grad = direct[rows, lanes]
+            now = u[rows, lanes]
+            earlier = u[pl.ds(pl.multiple_of(jnp.maximum(at - 8, 0), 8), ROWS), lanes]
+            total = grad * taps[0]
+            sums[0] = sums[0] + grad * now
+            sums[4] = sums[4] + grad
+            for k in range(1, 4):
+                kept = grad * wide(masks[k - 1, rows, :], width)
+                total = total + taps[k] * shifted_up(kept, afters[k - 1], k, below[k])
+                sums[k] = sums[k] + kept * shifted_down(now, earlier, k, inside[k])
+                afters[k - 1] = kept
+            parts[half] = total
+        low_rows = pl.ds(pl.multiple_of(tile * 16, 16), 16)
+        low_u[low_rows, lanes] = jnp.concatenate(parts, axis=0).astype(low_u.dtype)
+        return (*afters, *sums)
+
+    sums = lax.fori_loop(0, tiles, one, (nothing,) * 8, unroll=2)[3:]
+    for k in range(5):
+        tallies[k : k + 1, lanes] = jnp.sum(sums[k], axis=0, keepdims=True)
+
+
+def product_into(target, lanes, first, second, pieces, extra=None):
+    rows_in = first.shape[0] // pieces
+
+    def one(piece, carry):
+        rows = pl.ds(pl.multiple_of(piece * rows_in, rows_in), rows_in)
+        total = jnp.dot(first[rows, :], second, preferred_element_type=jnp.float32)
+        if extra is not None:
+            total = total + extra[rows, lanes].astype(jnp.float32)
+        target[rows, lanes] = total.astype(target.dtype)
+        return carry
+
+    lax.fori_loop(0, pieces, one, 0)
+
+
+def mixer_forward_kernel(
+    width, tokens, gain_one, gain_two, vec, masks, expand, gating, contract,
+    normed, u, branch, recur, inlet, conv, state, mixed, middle, normed_two,
+):
+    places, channels = u.shape
+    head = gating.shape[1] // 2
+    rms_rows(tokens, gain_one, normed, places)
+
+    def group(index, carry):
+        lanes = pl.ds(pl.multiple_of(index * width, width), width)
+        right = pl.ds(pl.multiple_of(channels + index * width, width), width)
+        product_into(u, lanes, normed, expand[:, lanes], 2)
+        product_into(branch, lanes, normed, expand[:, right], 2)
+        conv_forward(u, vec, masks, conv, lanes, width, places)
+        for part in range(width // head):
+            spot = pl.ds(pl.multiple_of(index * width + part * head, head), head)
+            logits = jnp.dot(conv[:, spot], gating[spot, :], preferred_element_type=jnp.float32)
+            recur[:, spot] = logits[:, :head]
+            inlet[:, spot] = logits[:, head:]
+        mix_forward(recur, inlet, branch, conv, vec, masks, state, mixed, lanes, width, places)
+        return carry
+
+    lax.fori_loop(0, channels // width, group, 0)
+
+    def column(index, carry):
+        lanes = pl.ds(pl.multiple_of(index * 256, 256), 256)
+        product_into(middle, lanes, mixed, contract[:, lanes], 2, tokens)
+        return carry
+
+    lax.fori_loop(0, middle.shape[1] // 256, column, 0)
+    rms_rows(middle, gain_two, normed_two, places)
+
+
+def mixer_forward(tokens, gain_one, gain_two, vec, masks, expand, gating, contract, width=256):
+    places, features = tokens.shape
+    channels = contract.shape[0]
+    wide_f32 = jax.ShapeDtypeStruct((places, channels), jnp.float32)
+    wide_low = jax.ShapeDtypeStruct((places, channels), BRAIN)
+    return pl.pallas_call(
+        functools.partial(mixer_forward_kernel, width),
+        out_shape=[
+            jax.ShapeDtypeStruct((places, features), BRAIN),
+            wide_f32, wide_f32, wide_f32, wide_f32, wide_low, wide_f32, wide_low,
+            jax.ShapeDtypeStruct((places, features), jnp.float32),
+            jax.ShapeDtypeStruct((places, features), BRAIN),
+        ],
+        compiler_params=pltpu.CompilerParams(vmem_limit_bytes=VMEM_BYTES),
+    )(tokens, gain_one, gain_two, vec, masks, expand, gating, contract)
+
+
+def mixer_backward_kernel(
+    width, low, contract, gating, vec, masks, u, branch, recur, inlet, conv, state,
+    low_p, gating_grad, tallies, grad, direct, low_r, low_i,
+):
+    places, channels = u.shape
+    head = gating.shape[1] // 2
+
+    def group(index, carry):
+        lanes = pl.ds(pl.multiple_of(index * width, width), width)
+        right = pl.ds(pl.multiple_of(channels + index * width, width), width)
+        total = lax.dot_general(
+            low[...], contract[lanes, :], (((1,), (1,)), ((), ())), preferred_element_type=jnp.float32
+        )
+        grad[...] = total
+        here = slice(0, width)
+        views = [v.at[:, lanes] for v in (recur, inlet, branch, conv, state)]
+        mix_backward(
+            grad, *views, vec.at[:, lanes], masks, low_r, low_i, direct,
+            low_p.at[:, right], tallies.at[:, lanes], here, width, places,
+        )
+        for part in range(width // head):
+            spot = slice(part * head, (part + 1) * head)
+            at = pl.ds(pl.multiple_of(index * width + part * head, head), head)
+            low_both = jnp.concatenate([low_r[:, spot], low_i[:, spot]], axis=1)
+            gating_grad[at, :] = lax.dot_general(
+                conv[:, at], low_both, (((0,), (0,)), ((), ())), preferred_element_type=jnp.float32
+            ).astype(gating_grad.dtype)
+            direct[:, spot] += lax.dot_general(
+                low_both, gating[at, :], (((1,), (1,)), ((), ())), preferred_element_type=jnp.float32
+            )
+        conv_backward(
+            direct, u.at[:, lanes], vec.at[:, lanes], masks, low_p.at[:, lanes], tallies.at[:, lanes],
+            here, width, places,
+        )
+        return carry
+
+    lax.fori_loop(0, channels // width, group, 0)
+
+
+def mixer_backward(low, contract, gating, vec, masks, u, branch, recur, inlet, conv, state, width=256):
+    places, channels = u.shape
+    return pl.pallas_call(
+        functools.partial(mixer_backward_kernel, width),
+        out_shape=[
+            jax.ShapeDtypeStruct((places, 2 * channels), BRAIN),
+            jax.ShapeDtypeStruct(gating.shape, BRAIN),
+            jax.ShapeDtypeStruct((8, channels), jnp.float32),
+        ],
+        scratch_shapes=[
+            pltpu.VMEM((places, width), jnp.float32),
+            pltpu.VMEM((places, width), jnp.float32),
+            pltpu.VMEM((places, width), BRAIN),
+            pltpu.VMEM((places, width), BRAIN),
+        ],
+        compiler_params=pltpu.CompilerParams(vmem_limit_bytes=VMEM_BYTES),
+    )(low, contract, gating, vec, masks, u, branch, recur, inlet, conv, state)
+
+
+def channel_rows(temporal_rows):
+    decay = temporal_rows[7:8]
+    power = -GATE_POWER * jax.nn.softplus(-decay)
+    slope = GATE_POWER * jax.nn.sigmoid(-decay)
+    return jnp.concatenate([temporal_rows, power, slope, jnp.zeros_like(temporal_rows)[:6]], axis=0)
+
+
+def keep_masks(lengths, length):
+    starts = jnp.cumsum(lengths) - lengths
     places = jnp.arange(length, dtype=jnp.int32)
-    matches = places[:, None] == starts[..., None, :]
-    resets = jnp.any(matches, axis=-1).astype(jnp.float32)
-    segment = jnp.sum((starts[..., None, :] <= places[:, None]).astype(jnp.int32), axis=-1)
-    return (resets, segment)
-
-
-def causal_conv(inputs, conv_taps, conv_bias, segment):
-    length = inputs.shape[-2]
-    running = conv_bias + inputs * conv_taps[:, 0]
-    for offset in range(1, 4):
-        shifted = jnp.concatenate(
-            [jnp.zeros_like(inputs[..., :offset, :]), inputs[..., : length - offset, :]], axis=-2
-        )
-        earlier_segment = jnp.concatenate(
-            [jnp.full_like(segment[..., :offset], -1), segment[..., : length - offset]], axis=-1
-        )
-        keeping = (earlier_segment == segment).astype(jnp.float32)[..., None]
-        running = running + shifted * conv_taps[:, offset] * keeping
-    return running
-
-
-def combine_linear(earlier, later):
-    return (earlier[0] * later[0], later[0] * earlier[1] + later[1])
-
-
-def recurrence(decays, inputs):
-    return lax.associative_scan(combine_linear, (decays, inputs), axis=-2)[1]
-
-
-def temporal_mix(gate_logits, branch_logits, conv_values, recur_bias, resets):
-    head_width = gate_logits.shape[-1] // 2
-    flat_shape = branch_logits.shape
-    recur_logit = gate_logits[..., :head_width].reshape(flat_shape) + recur_bias[:, 0]
-    input_logit = gate_logits[..., head_width:].reshape(flat_shape) + recur_bias[:, 1]
-    recur_gate = jax.nn.sigmoid(recur_logit)
-    input_gate = jax.nn.sigmoid(input_logit)
-    log_decay = -GATE_POWER * recur_gate * jax.nn.softplus(-recur_bias[:, 2])
-    carried = 1.0 - resets[..., None]
-    decays = jnp.exp(log_decay) * carried
-    scaling = jnp.sqrt(-jnp.expm1(2.0 * log_decay)) * carried + resets[..., None]
-    states = recurrence(decays, scaling * input_gate * conv_values)
-    return states * jax.nn.gelu(branch_logits)
+    resets = jnp.any(places[:, None] == starts[None, :], axis=-1)
+    one = 1.0 - resets.astype(jnp.float32)
+    two = one * jnp.concatenate([jnp.zeros((1,)), one[:-1]])
+    three = two * jnp.concatenate([jnp.zeros((2,)), one[:-2]])
+    return jnp.broadcast_to(jnp.stack([one, two, three])[:, :, None], (3, length, LANES))
+
+
+def rms_pull(values, gain, grad):
+    scale = lax.rsqrt(jnp.mean(values * values, axis=-1, keepdims=True) + NORM_EPSILON)
+    scaled = grad * gain
+    inner = jnp.mean(values * scaled, axis=-1, keepdims=True)
+    return scale * scaled - values * (scale * scale * scale * inner), jnp.sum(grad * values * scale, axis=0)
 
 
 def product_rows(former, latter):
@@ -479,91 +785,47 @@
     vectors = vectors.reshape(-1, 8, 128).transpose(0, 2, 1)
     temporal_float = vectors[:, :rows_t].reshape(-1, 8)
     scales_float = vectors[:, rows_t : rows_t + rows_s, :2].reshape(-1, 2)
-    width = contract_full.shape[0]
     hidden = narrow_full.shape[0]
-    head_width = gating_full.shape[1] // 2
-    head_count = width // head_width
     length = tokens.shape[1]
-    resets, segment = doc_tables(doc_lengths, length)
-    resets = resets[0]
-    segment = segment[0]
-    inputs = tokens[0].astype(jnp.float32)
-    normed, norm_pull = jax.vjp(rms_scale, inputs, scales_float[:, 0])
-    normed_low = normed.astype(brain)
-    projected = jnp.dot(normed_low, expand_full, preferred_element_type=jnp.float32)
-
-    def conv_piece(values, conv_taps, conv_bias):
-        return causal_conv(values, conv_taps, conv_bias, segment)
-
-    conv_out, conv_pull = jax.vjp(
-        conv_piece, projected[:, :width], temporal_float[:, 0:4], temporal_float[:, 4]
-    )
-    conv_low = conv_out.astype(brain)
-    blocks = conv_low.reshape(length, head_count, head_width)
-    gate_logits = jnp.einsum(
-        "lhk,hkj->lhj",
-        blocks,
-        gating_full.reshape(head_count, head_width, 2 * head_width),
-        preferred_element_type=jnp.float32,
-    )
-
-    def mix_piece(logits, branch_logits, conv_values, recur_bias):
-        return temporal_mix(logits, branch_logits, conv_values, recur_bias, resets)
-
-    mixed, mix_pull = jax.vjp(
-        mix_piece,
-        gate_logits,
-        projected[:, width:],
-        conv_low.astype(jnp.float32),
-        temporal_float[:, 5:8],
-    )
-    mixed_low = mixed.astype(brain)
-    middle = inputs + jnp.dot(mixed_low, contract_full, preferred_element_type=jnp.float32)
-    normed_two, norm_two_pull = jax.vjp(rms_scale, middle, scales_float[:, 1])
-    normed_two_low = normed_two.astype(brain)
-    widened = jnp.dot(normed_two_low, widen_full, preferred_element_type=jnp.float32)
-
-    def gated_piece(values):
-        return jax.nn.gelu(values[:, :hidden]) * values[:, hidden:]
-
-    activated, gated_pull = jax.vjp(gated_piece, widened)
-    activated_low = activated.astype(brain)
+    inputs = tokens[0]
+    vec = channel_rows(temporal_float.T)
+    masks = keep_masks(doc_lengths[0], length)
+    gains = scales_float.T
+    normed, u, branch, recur, inlet, conv, state, mixed, middle, normed_two = mixer_forward(
+        inputs, gains[0:1], gains[1:2], vec, masks, expand_full, gating_full, contract_full
+    )
+    widened = jnp.dot(normed_two, widen_full, preferred_element_type=jnp.float32)
+    gate, up = widened[:, :hidden], widened[:, hidden:]
+    half, slope = gelu_parts(gate)
+    activated = (gate * half * up).astype(brain)
     block_out = (
-        middle + jnp.dot(activated_low, narrow_full, preferred_element_type=jnp.float32)
+        middle + jnp.dot(activated, narrow_full, preferred_element_type=jnp.float32)
     ).astype(brain)
     upstream = cotangent[0]
-    narrow_grad = product_rows(activated_low, upstream)
+    narrow_grad = product_rows(activated, upstream)
     activated_grad = product_cols(upstream, narrow_full)
-    widened_grad = gated_pull(activated_grad)[0].astype(brain)
-    widen_grad = product_rows(normed_two_low, widened_grad)
+    widened_grad = jnp.concatenate(
+        [activated_grad * up * slope, activated_grad * (gate * half)], axis=1
+    ).astype(brain)
+    widen_grad = product_rows(normed_two, widened_grad)
     normed_two_grad = product_cols(widened_grad, widen_full)
-    middle_norm_grad, scale_two_grad = norm_two_pull(normed_two_grad)
+    middle_norm_grad, scale_two_grad = rms_pull(middle, gains[1], normed_two_grad)
     middle_grad = upstream.astype(jnp.float32) + middle_norm_grad
     middle_low = middle_grad.astype(brain)
-    contract_grad = product_rows(mixed_low, middle_low)
-    mixed_grad = product_cols(middle_low, contract_full)
-    logit_grad, branch_grad, conv_mix_grad, recur_bias_grad = mix_pull(mixed_grad)
-    logit_low = logit_grad.astype(brain)
-    gating_blocks = gating_full.reshape(head_count, head_width, 2 * head_width)
-    gating_grad = jnp.einsum(
-        "lhk,lhj->hkj", blocks, logit_low, preferred_element_type=jnp.float32
-    ).reshape(width, 2 * head_width)
-    conv_grad = conv_mix_grad + jnp.einsum(
-        "lhj,hkj->lhk", logit_low, gating_blocks, preferred_element_type=jnp.float32
-    ).reshape(length, width)
-    input_grad, taps_grad, conv_bias_grad = conv_pull(conv_grad)
-    projected_low = jnp.concatenate([input_grad, branch_grad], axis=1).astype(brain)
-    expand_grad = product_rows(normed_low, projected_low)
+    contract_grad = product_rows(mixed, middle_low)
+    projected_low, gating_grad, temporal_grad = mixer_backward(
+        middle_low, contract_full, gating_full, vec, masks, u, branch, recur, inlet, conv, state
+    )
+    expand_grad = product_rows(normed, projected_low)
     normed_grad = product_cols(projected_low, expand_full)
-    token_norm_grad, scale_one_grad = norm_pull(normed_grad)
+    token_norm_grad, scale_one_grad = rms_pull(inputs.astype(jnp.float32), gains[0], normed_grad)
     tokens_grad = (middle_grad + token_norm_grad).astype(brain)
-    scales_grad = jnp.stack([scale_one_grad, scale_two_grad], axis=1)
-    temporal_grad = jnp.concatenate([taps_grad, conv_bias_grad[:, None], recur_bias_grad], axis=1)
+    scales_grad = jnp.stack([scale_one_grad, scale_two_grad])
     devices = 1 << cube.bits
     misc = jnp.concatenate(
         [
-            temporal_grad.T.reshape(8, devices, rows_t),
-            jnp.pad(scales_grad.T, ((0, 6), (0, 0))).reshape(8, devices, rows_s),
+            temporal_grad.reshape(8, devices, rows_t),
+            jnp.pad(scales_grad, ((0, 6), (0, 0))).reshape(8, devices, rows_s),
         ],
         axis=2,
     )

time: 917 us -> 479 us (0.52)
  local copies, waits for them, and re-layouts: 357 us -> 18.9 us
  other arithmetic: 147 us -> 11.2 us
  Pallas kernels: 287 us -> 365 us
  matrix products: 113 us -> 79.2 us
    pad x71 -> x0, local copies, waits for them, and re-layouts: 169 us -> none  [the longest x70 169 us: recurrence(): return lax.associative_scan(combine_linear, (decays, inputs), axis=-2)[1]]
    slice x74 -> x2, local copies, waits for them, and re-layouts: 137 us -> 0.61 us  [the longest x1 0.61 us: shards(): gains[1:2]]
    pallas_call x0 -> x2, Pallas kernels: none -> 77.6 us  [the longest x1 43.4 us: mixer_forward(): pl.pallas_call(functools.partial(mixer_forward_kernel, width), out_shape=...]
    mul x19 -> x5, other arithmetic: 31.8 us -> 0.23 us  [the longest x1 0.08 us: keep_masks(): three = two * jnp.concatenate([jnp.zeros((2,)), one[:-2]])]
    reduce_sum x7 -> x2, other arithmetic: 29.9 us -> 0.49 us  [rms_pull(): jnp.mean(values * values, axis=-1, keepdims=True) + NORM_EPSILON]
    add_any x18 -> x0, other arithmetic: 24 us -> none  [the longest x8 21.5 us: combine_linear(): return (earlier[0] * later[0], later[0] * earlier[1] + later[1])]
    add x18 -> x0, other arithmetic: 21.9 us -> none  [the longest x9 11.4 us: combine_linear(): return (earlier[0] * later[0], later[0] * earlier[1] + later[1])]
    dot_general x7 -> x2, matrix products: 38.5 us -> 17.2 us  [the longest x1 12.7 us: shards(): jnp.dot(normed_two, widen_full, preferred_element_type=jnp.float32)]
where the time goes in v2:
time: 479 us; the launch traced here: 475 us
  Pallas kernels  365 us (76%)
  matrix products  79.2 us (17%)
  local copies, waits for them, and re-layouts  18.9 us (4%)
  other arithmetic  11.2 us (2%)
    pallas_call x1, Pallas kernels, scatter_all(): pl.pallas_call(functools.partial(scatter_kernel, cube, pieces, count), ou...  147 us
    pallas_call x1, Pallas kernels, gather_all(): pl.pallas_call(functools.partial(gather_kernel, cube, pieces, count), out...  133 us
    pallas_call x1, Pallas kernels, mixer_forward(): pl.pallas_call(functools.partial(mixer_forward_kernel, width), out_shape=...  43.4 us
    dot_general x3, matrix products, product_cols(): lax.dot_general(former, latter, (((1,), (1,)), ((), ())), preferred_eleme...  34.9 us
    pallas_call x1, Pallas kernels, mixer_backward(): pl.pallas_call(functools.partial(mixer_backward_kernel, width), out_shape...  34.2 us
    dot_general x4, matrix products, product_rows(): lax.dot_general(former, latter, (((0,), (0,)), ((), ())), preferred_eleme...  27.1 us
    unnamed x60, local copies, waits for them, and re-layouts  12.8 us
    dot_general x1, matrix products, shards(): jnp.dot(normed_two, widen_full, preferred_element_type=jnp.float32)  12.7 us

profile of v2, /device:TPU:0, one launch (start us, length us, event | category | flops | bytes accessed | tf_op | source)
XLA Modules:
  0.0 475.0 jit_solution(4491941919584589827)
XLA Ops:
  1.3 0.7 convert_bitcast_fusion
  2.7 132.9 %shard_map.415 = (f32[2,2,2,2,2,8,128]{6,5,4,3,2,1,0:T(8,128)}, bf16[2,2,2,2,2,32,3072]{6,5,4,3,2,1,0:T(8,128)(2,1)}, bf16[2,2,2,2,2,48,256]{6,5,4,3,2,1,0:T(8,1...) custom-call(f32[8,128]{1,0:T(8,128)} %pad_convert_fusion.refs_0_, ...), custom_call_target="tpu_custom_call" | custom-call | tf_op jit(solution)/shard_map/pallas_call | solution.py:137
  135.6 0.9 copy.103
  137.6 0.7 maximum_maximum_fusion.vec
  138.3 0.8 reduce-window_clone.1
  140.1 1.1 broadcast_in_dim.6.masks
  141.2 43.4 %shard_map.416 = (bf16[512,1024]{1,0:T(8,128)(2,1)}, f32[512,1536]{1,0:T(8,128)}, f32[512,1536]{1,0:T(8,128)}, f32[512,1536]{1,0:T(8,128)}, f32[512,1536]{1,0:T(...) custom-call(bf16[512,1024]{1,0:T(8,128)(2,1)} %bitcast.91, ...), custom_call_target="tpu_custom_call" | custom-call | tf_op jit(solution)/shard_map/pallas_call | solution.py:636
  184.6 12.7 %fusion.28 = f32[512,6144]{1,0:T(8,128)} fusion(bf16[512,1024]{1,0:T(8,128)(2,1)} %get-tuple-element.77, bf16[1024,6144]{1,0:T(8,128)(2,1)} %bitcast.122), kind=kOutput, calls=%fused_computation.71 | convolution fusion | flops 6442450944 | bytes 26214400 | tf_op jit(solution)/shard_map/dot_general | solution.py:797
  197.4 13.6 %fusion.1 = (bf16[512,3072]{1,0:T(8,128)(2,1)}, bf16[512,3072]{1,0:T(8,128)(2,1)}, bf16[512,3072]{1,0:T(8,128)(2,1)S(1)}) fusion(f32[512,6144]{1,0:T(8,128)} %fusion.28, bf16[3072,1024]{1,0:T(8,128)(2,1)} %bitcast.124, bf16[1,512,1024]{2,1,0:T(8,128)(2,1)S(1)} %copy-done.3), kind=kOutput, calls=%fused_computation.5 | convolution fusion | flops 3255828480 | bytes 29360128 | tf_op jit(solution)/shard_map/dot_general | solution.py:737
  211.0 4.4 fusion.12
  215.7 14.0 %multiply_reduce_fusion = (f32[1024]{0:T(1024)S(1)}, f32[512]{0:T(512)S(1)}, f32[512,1024]{1,0:T(8,128)}) fusion(f32[512,1024]{1,0:T(8,128)S(1)} %copy-done, f32[512]{0:T(512)S(1)} %add_rsqrt_fusion.1, f32[1024]{0:T(1024)S(1)} %bitcast.112, bf16[1024,6144]{1,0:T(8,128)(2,1)} %bitcast.123, bf16[512,3072]{1,0:T(8,128)(2,1)} %get-tuple-element.197, ...), kind=kOutput, calls=%fused_computation.27 | convolution fusion | flops 6458178048 | bytes 23080960 | tf_op jit(solution)/shard_map/dot_general | solution.py:737
  230.0 3.3 fusion.26.low
  233.4 34.2 %shard_map.417 = (bf16[512,3072]{1,0:T(8,128)(2,1)}, bf16[1536,256]{1,0:T(8,128)(2,1)}, f32[8,1536]{1,0:T(8,128)}) custom-call(bf16[512,1024]{1,0:T(8,128)(2,1)} %fusion.26.low, bf16[1536,1024]{1,0:T(8,128)(2,1)} %bitcast.90, bf16[1536,256]{1,0:T(8,128)(2,1)} %bitcast.98, f32[16,1536]{1,0:T(8,128)} %maximum_maximum_fusion.vec, ...), custom_call_target="tpu_custom_call" | custom-call | tf_op jit(solution)/shard_map/pallas_call | solution.py:689
  267.6 7.3 %fusion.11 = (f32[1024]{0:T(1024)S(1)}, f32[512]{0:T(512)S(1)}, f32[512,1024]{1,0:T(8,128)S(1)}) fusion(f32[512]{0:T(512)S(1)} %get-tuple-element.206, bf16[1,512,1024]{2,1,0:T(8,128)(2,1)S(1)} %copy-done.1, f32[1024]{0:T(1024)S(1)} %bitcast.115, bf16[512,3072]{1,0:T(8,128)(2,1)} %get-tuple-element.86, bf16[1024,3072]{1,0:T(8,128)(2,1)} %bitcast.95), kind=kOutput, calls=%fused_computation.26 | convolution fusion | flops 3224893952 | bytes 12595200 | tf_op jit(solution)/shard_map/dot_general | solution.py:737
  275.0 2.0 fusion.13
  277.3 0.8 select_maximum_fusion
  278.1 8.4 %convolution_convert_fusion.2 = bf16[1024,3072]{1,0:T(8,128)(2,1)} fusion(bf16[512,1024]{1,0:T(8,128)(2,1)} %get-tuple-element.88, bf16[512,3072]{1,0:T(8,128)(2,1)} %get-tuple-element.86), kind=kOutput, calls=%fused_computation.13 | convolution fusion | flops 3224371200 | bytes 10485760 | tf_op jit(solution)/shard_map/dot_general | solution.py:731
  286.5 3.5 convolution_convert_fusion.3
  290.4 9.8 %convolution_convert_fusion = bf16[1024,6144]{1,0:T(8,128)(2,1)} fusion(bf16[512,1024]{1,0:T(8,128)(2,1)S(1)} %copy-done.17, bf16[512,3072]{1,0:T(8,128)(2,1)S(1)} %copy-done.19, bf16[512,3072]{1,0:T(8,128)(2,1)S(1)} %copy-done.18), kind=kOutput, calls=%fused_computation | convolution fusion | flops 6461325312 | bytes 19922944 | tf_op jit(solution)/shard_map/dot_general | solution.py:731
  300.2 5.4 %convolution_convert_fusion.1 = bf16[3072,1024]{1,0:T(8,128)(2,1)} fusion(bf16[512,3072]{1,0:T(8,128)(2,1)S(1)} %copy-done.21, bf16[1,512,1024]{2,1,0:T(8,128)(2,1)S(1)} %copy-done.5), kind=kOutput, calls=%fused_computation.12 | convolution fusion | flops 3224371200 | bytes 10485760 | tf_op jit(solution)/shard_map/dot_general | solution.py:731
  305.6 146.9 %shard_map.418 = (f32[8,128]{1,0:T(8,128)}, f32[32,3072]{1,0:T(8,128)}, f32[48,256]{1,0:T(8,128)}, f32[48,1024]{1,0:T(8,128)}, f32[32,6144]{1,0:T(8,128)}, /*index=5*/f32[96,1024]{1,0:T(8,128)}, f32[8,128]{1,0:T(8,128)}) custom-call(f32[2,2,2,2,2,8,128]{6,5,4,3,2,1,0:T(8,128)} %bitcast.102, bf16[2,2,2,2,2,32,3072]{6,5,4,3,2,1,0:T(8,128)(2,1)} %bitcast.92, ...), custom_call_target="tpu_custom_call" | custom-call | tf_op jit(solution)/shard_map/pallas_call | solution.py:277
  452.6 0.8 copy.87
  453.9 1.4 copy.88
  458.0 0.7 copy.93.refs_26_
  458.7 0.7 copy.94.refs_27_
  459.4 7.0 %shard_map.419 = (f32[1,1]{1,0:T(1,128)}, f32[32,3072]{1,0:T(8,128)}, f32[48,256]{1,0:T(8,128)}, f32[48,1024]{1,0:T(8,128)}, f32[32,6144]{1,0:T(8,128)}, /*index...) custom-call(f32[8,128]{1,0:T(8,128)} %get-tuple-element.91.norm_tile, ...), custom_call_target="tpu_custom_call" | custom-call | tf_op jit(solution)/shard_map/pallas_call | solution.py:362
  466.4 1.4 copy.95
  467.8 1.4 copy.96
  469.1 1.4 copy.97
  470.5 1.4 copy.98
  471.9 1.4 copy.99
  473.3 1.4 copy.100
  (80 shorter events, 7.9 us)
Async XLA Ops:
  184.6 12.7 %copy-start.3 = (bf16[1,512,1024]{2,1,0:T(8,128)(2,1)S(1)}, bf16[1,512,1024]{2,1,0:T(8,128)(2,1)}, u32[]{:S(2)}) copy-start(bf16[1,512,1024]{2,1,0:T(8,128)(2,1)} %param.25) | copy-start | bytes 3145732
  184.6 26.4 %slice-start = ((s8[6291456]{0:T(1024)(128)(4,1)}), s8[4194304]{0:T(1024)(128)(4,1)S(1)}, s32[]{:S(2)}) async-start(s8[6291456]{0:T(1024)(128)(4,1)} %bitcast.125), calls=%async_computation | async-start | bytes 8388608
  197.4 13.6 %copy-start = (f32[512,1024]{1,0:T(8,128)S(1)}, f32[512,1024]{1,0:T(8,128)}, u32[]{:S(2)}) copy-start(f32[512,1024]{1,0:T(8,128)} %get-tuple-element.76) | copy-start | bytes 6291460
  197.4 13.6 %slice-start.1 = ((s8[6291456]{0:T(1024)(128)(4,1)}), s8[2097152]{0:T(1024)(128)(4,1)S(1)}, s32[]{:S(2)}) async-start(s8[6291456]{0:T(1024)(128)(4,1)} %bitcast.125), calls=%async_computation.1 | async-start | bytes 4194304
  211.0 4.5 copy-start.20
  211.0 4.7 copy-start.7
  215.7 14.0 %copy-start.1 = (bf16[1,512,1024]{2,1,0:T(8,128)(2,1)S(1)}, bf16[1,512,1024]{2,1,0:T(8,128)(2,1)}, u32[]{:S(2)}) copy-start(bf16[1,512,1024]{2,1,0:T(8,128)(2,1)} %param.24) | copy-start | bytes 3145732
  233.4 34.2 %copy-start.9 = (f32[1,1024]{1,0:T(1,128)S(1)}, f32[1,1024]{1,0:T(1,128)}, u32[]{:S(2)}) copy-start(f32[1,1024]{1,0:T(1,128)} %get-tuple-element.202.gain_one) | copy-start | bytes 12292
  267.6 7.3 %copy-start.2 = (f32[512,1024]{1,0:T(8,128)S(1)}, f32[512,1024]{1,0:T(8,128)}, u32[]{:S(2)}) copy-start(f32[512,1024]{1,0:T(8,128)} %get-tuple-element.203) | copy-start | bytes 6291460
  267.6 7.3 %copy-start.4 = (bf16[1,512,1024]{2,1,0:T(8,128)(2,1)S(1)}, bf16[1,512,1024]{2,1,0:T(8,128)(2,1)}, u32[]{:S(2)}) copy-start(bf16[1,512,1024]{2,1,0:T(8,128)(2,1)} %param.25) | copy-start | bytes 3145732
  275.0 2.2 copy-start.8
  278.1 8.4 %copy-start.6 = (bf16[512,1024]{1,0:T(8,128)(2,1)S(1)}, bf16[512,1024]{1,0:T(8,128)(2,1)}, u32[]{:S(2)}) copy-start(bf16[512,1024]{1,0:T(8,128)(2,1)} %fusion.26.low) | copy-start | bytes 3145732
  278.1 8.4 %copy-start.16 = (bf16[512,1536]{1,0:T(8,128)(2,1)S(1)}, bf16[512,1536]{1,0:T(8,128)(2,1)}, u32[]{:S(2)}) copy-start(bf16[512,1536]{1,0:T(8,128)(2,1)} %get-tuple-element.90) | copy-start | bytes 4718596
  286.5 3.6 copy-start.17
  286.5 3.6 copy-start.18
  286.5 3.9 copy-start.19
  290.4 9.8 %copy-start.5 = (bf16[1,512,1024]{2,1,0:T(8,128)(2,1)S(1)}, bf16[1,512,1024]{2,1,0:T(8,128)(2,1)}, u32[]{:S(2)}) copy-start(bf16[1,512,1024]{2,1,0:T(8,128)(2,1)} %param.25) | copy-start | bytes 3145732
  290.4 9.8 %copy-start.21 = (bf16[512,3072]{1,0:T(8,128)(2,1)S(1)}, bf16[512,3072]{1,0:T(8,128)(2,1)}, u32[]{:S(2)}) copy-start(bf16[512,3072]{1,0:T(8,128)(2,1)} %copy-done.20) | copy-start | bytes 9437188
  305.6 149.7 %copy-start.13 = (f32[32,2]{0,1:T(2,128)S(1)}, f32[32,2]{0,1:T(2,128)}, u32[]{:S(2)}) copy-start(f32[32,2]{0,1:T(2,128)} %param.42) | copy-start | bytes 772
  305.6 150.4 %copy-start.10 = (f32[48,8]{0,1:T(8,128)S(1)}, f32[48,8]{0,1:T(8,128)}, u32[]{:S(2)}) copy-start(f32[48,8]{0,1:T(8,128)} %param.45) | copy-start | bytes 4612
  305.6 151.1 %copy-start.14 = (f32[32,2]{0,1:T(2,128)S(1)}, f32[32,2]{0,1:T(2,128)}, u32[]{:S(2)}) copy-start(f32[32,2]{0,1:T(2,128)} %param.43) | copy-start | bytes 772
  305.6 151.8 %copy-start.11 = (f32[48,8]{0,1:T(8,128)S(1)}, f32[48,8]{0,1:T(8,128)}, u32[]{:S(2)}) copy-start(f32[48,8]{0,1:T(8,128)} %param.46) | copy-start | bytes 4612
  305.6 152.5 %copy-start.15 = (f32[32,2]{0,1:T(2,128)S(1)}, f32[32,2]{0,1:T(2,128)}, u32[]{:S(2)}) copy-start(f32[32,2]{0,1:T(2,128)} %param.44) | copy-start | bytes 772
  305.6 153.1 %copy-start.12 = (f32[48,8]{0,1:T(8,128)S(1)}, f32[48,8]{0,1:T(8,128)}, u32[]{:S(2)}) copy-start(f32[48,8]{0,1:T(8,128)} %param.47) | copy-start | bytes 4612
